TPU v7x, 256 devices: a whole 4x4x8 slice. The times are simulated.
256 devices in a mesh: ctx: 32 (over z, x_lo, core), head: 8 (over y, x_hi).
Axes of the slice: x: 4 (x_hi: 2, x_lo: 2; x = x_hi * 2 + x_lo), y: 4, z: 8, core: 2. Of those that a mesh axis runs over, the one named last changes fastest.
Arguments:
- queries: bfloat16 [4096, 12288], P('ctx', 'head'), may hold values from -8 to 8
- compressed: bfloat16 [4096, 576], P('ctx'), may hold values from -16 to 16
- latent_gain: float32 [512], replicated, may hold values from 0.25 to 1.75
- w_uk: bfloat16 [512, 8192], P(None, 'head'), may hold values from -0.25 to 0.25
- w_uv: bfloat16 [512, 8192], P(None, 'head'), may hold values from -0.25 to 0.25
- w_out: bfloat16 [8192, 7168], P('head', 'ctx'), may hold values from -0.5 to 0.5
Outputs:
- output: bfloat16 [4096, 7168], P('ctx', 'head')
All inputs are finite; a program needn't handle non-finite values.
Results may differ from a plain program's by a relative error of at most 0.018.
Values may be sent and summed in bfloat16 or wider, within the bound.
A program may use at most 64 MiB of HBM per device.

v0:
```python
import jax
import jax.numpy as jnp
from jax import lax
from jax.sharding import PartitionSpec as P

LATENT = 512
ROPE = 64
NOPE = 128


def passed_along(block, axis, distance):
    devices = range(lax.axis_size(axis))
    route = [((i - distance) % len(devices), i) for i in devices]
    return lax.ppermute(block, axis, route)


def compress_norm(compressed, latent_gain):
    latent = compressed[:, :LATENT].astype(jnp.float32)
    mean_square = jnp.mean(latent * latent, axis=1, keepdims=True)
    normed = (latent * lax.rsqrt(mean_square + 1e-06) * latent_gain).astype(jnp.bfloat16)
    return jnp.concatenate([normed, compressed[:, LATENT:]], axis=1)


def place_rows(owner_rank, row_count):
    offsets = jnp.arange(row_count, dtype=jnp.int32)
    return owner_rank * row_count + offsets


def empty_state(row_count, head_count):
    return (
        jnp.full((row_count, head_count), -jnp.inf, jnp.float32),
        jnp.zeros((row_count, head_count), jnp.float32),
        jnp.zeros((row_count, head_count, NOPE), jnp.float32),
    )


def attend_quarter(part_state, query_part, query_pos, keys_content, keys_rotary, values, key_pos):
    running_max, running_sum, running_out = part_state
    head_count = keys_content.shape[1]
    shaped = query_part.reshape(query_part.shape[0], head_count, NOPE + ROPE)
    scores = jnp.einsum(
        "qhd,khd->qhk", shaped[:, :, :NOPE], keys_content, preferred_element_type=jnp.float32
    )
    scores = scores + jnp.einsum(
        "qhd,kd->qhk", shaped[:, :, NOPE:], keys_rotary, preferred_element_type=jnp.float32
    )
    scores = scores * (NOPE + ROPE) ** (-0.5)
    visible = query_pos[:, None] >= key_pos[None, :]
    scores = jnp.where(visible[:, None, :], scores, -jnp.inf)
    new_max = jnp.maximum(running_max, jnp.max(scores, axis=2))
    probabilities = jnp.exp(scores - new_max[:, :, None])
    rescale = jnp.exp(running_max - new_max)
    new_sum = running_sum * rescale + jnp.sum(probabilities, axis=2)
    weighted = jnp.einsum(
        "qhk,khd->qhd",
        probabilities.astype(jnp.bfloat16),
        values,
        preferred_element_type=jnp.float32,
    )
    new_out = running_out * rescale[:, :, None] + weighted
    return (new_max, new_sum, new_out)


def keep_state(part_state, *unused):
    return part_state


def attend_block(softmax_state, query_rows, query_pos, latent_block, key_pos, w_uk, w_uv):
    key_count = latent_block.shape[0]
    head_count = w_uk.shape[1] // NOPE
    latent = latent_block[:, :LATENT]
    keys_content = (
        jnp.dot(latent, w_uk, preferred_element_type=jnp.float32)
        .astype(jnp.bfloat16)
        .reshape(key_count, head_count, NOPE)
    )
    values = (
        jnp.dot(latent, w_uv, preferred_element_type=jnp.float32)
        .astype(jnp.bfloat16)
        .reshape(key_count, head_count, NOPE)
    )
    keys_rotary = latent_block[:, LATENT:]
    rows_half = query_rows.shape[0] // 2
    keys_half = key_count // 2
    updated = []
    for query_half in range(2):
        row_start = query_half * rows_half
        row_stop = row_start + rows_half
        part_state = softmax_state[query_half]
        for key_half in range(2):
            key_start = key_half * keys_half
            key_stop = key_start + keys_half
            visible_any = key_pos[key_start] <= query_pos[row_stop - 1]
            part_state = lax.cond(
                visible_any,
                attend_quarter,
                keep_state,
                part_state,
                query_rows[row_start:row_stop],
                query_pos[row_start:row_stop],
                keys_content[key_start:key_stop],
                keys_rotary[key_start:key_stop],
                values[key_start:key_stop],
                key_pos[key_start:key_stop],
            )
        updated.append(part_state)
    return tuple(updated)


def on_device(queries, compressed, latent_gain, w_uk, w_uv, w_out):
    cycle_size = lax.axis_size("ctx")
    device_index = lax.axis_index("ctx")
    row_count = queries.shape[0]
    halfway = row_count // 2
    head_count = w_uk.shape[1] // NOPE
    latent_block = compress_norm(compressed, latent_gain)
    query_pos = place_rows(device_index, row_count)
    softmax_state = (empty_state(halfway, head_count), empty_state(halfway, head_count))

    def pass_turn(turn_index, carry):
        current_block, states = carry
        source_rank = (device_index + turn_index) % cycle_size
        key_pos = place_rows(source_rank, row_count)
        states = attend_block(states, queries, query_pos, current_block, key_pos, w_uk, w_uv)
        current_block = passed_along(current_block, "ctx", -1)
        return (current_block, states)

    latent_block, softmax_state = lax.fori_loop(
        0, cycle_size - 1, pass_turn, (latent_block, softmax_state)
    )
    last_rank = (device_index - 1) % cycle_size
    softmax_state = attend_block(
        softmax_state,
        queries,
        query_pos,
        latent_block,
        place_rows(last_rank, row_count),
        w_uk,
        w_uv,
    )
    halves = [part_state[2] / part_state[1][:, :, None] for part_state in softmax_state]
    attention = (
        jnp.concatenate(halves, axis=0).reshape(row_count, head_count * NOPE).astype(jnp.bfloat16)
    )
    partial_rows = jnp.dot(
        attention,
        lax.all_gather(w_out, "ctx", axis=1, tiled=True),
        preferred_element_type=jnp.float32,
    )
    return lax.psum_scatter(
        partial_rows.astype(jnp.bfloat16), "head", scatter_dimension=1, tiled=True
    )


def solution(mesh):
    return jax.shard_map(
        on_device,
        mesh=mesh,
        in_specs=(
            P("ctx", "head"),
            P("ctx", None),
            P(),
            P(None, "head"),
            P(None, "head"),
            P("head", "ctx"),
        ),
        out_specs=P("ctx", "head"),
        check_vma=False,
    )
```

profile of v0, /device:TPU:239, one launch (start us, length us, event | category | flops | bytes accessed | tf_op | source)
XLA Modules:
  0.0 617.8 jit_solution(10663841379484234659)
XLA Ops:
  16.0 496.4 %while.27 = (s32[]{:T(128)}, bf16[128,576]{1,0:T(8,128)(2,1)S(1)}, f32[64,8]{0,1:T(8,128)S(1)}, f32[64,8]{0,1:T(8,128)S(1)}, f32[64,8,128]{2,0,1:T(8,128)S(1)}, ...) while((s32[]{:T(128)}, bf16[128,576]{1,0:T(8,128)(2,1)S(1)}, ...), condition=%wide.region_18.19_spmd, body=%wide.region_1.18_spmd.sunk | while | flops 354177152 | bytes 16586110 | solution.py:128
  24.9 1.6 convolution_convert_fusion.8
  38.4 1.5 convolution_convert_fusion.7
  40.0 1.6 convolution_convert_fusion.8
  72.2 1.6 convolution_convert_fusion.8
  88.2 1.6 convolution_convert_fusion.8
  104.3 1.5 convolution_convert_fusion.8
  120.3 1.5 convolution_convert_fusion.8
  136.3 1.5 convolution_convert_fusion.8
  152.3 1.5 convolution_convert_fusion.8
  168.4 1.5 convolution_convert_fusion.8
  184.4 1.5 convolution_convert_fusion.8
  232.4 1.5 convolution_convert_fusion.8
  248.4 1.5 convolution_convert_fusion.8
  264.5 1.5 convolution_convert_fusion.8
  280.5 1.5 convolution_convert_fusion.8
  296.5 1.5 convolution_convert_fusion.8
  312.5 1.5 convolution_convert_fusion.8
  328.5 1.5 convolution_convert_fusion.8
  376.6 1.5 convolution_convert_fusion.8
  392.6 1.5 convolution_convert_fusion.8
  408.6 1.5 convolution_convert_fusion.8
  424.6 1.5 convolution_convert_fusion.8
  440.6 1.5 convolution_convert_fusion.8
  456.7 1.5 convolution_convert_fusion.8
  472.7 1.5 convolution_convert_fusion.8
  514.0 1.5 convolution_convert_fusion.3
  520.7 1.6 conditional.11
  522.7 10.1 %convolution_convert_fusion.2 = bf16[128,7168]{1,0:T(8,128)(2,1)S(1)} fusion(bf16[128,1024]{0,1:T(8,128)(2,1)S(1)} %bitcast.170, bf16[1024,7168]{0,1:T(8,128)(2,1)} %all-gather.2.cloned.1.call-done), kind=kOutput, calls=%fused_computation.153 | convolution fusion | flops 1879965696 | bytes 16777216 | tf_op jit(solution)/shard_map/dot_general | solution.py:145
  532.8 2.3 copy.129
  535.2 74.0 %reduce-scatter.4.cloned.1.call-done = bf16[896,128]{1,0:T(8,128)(2,1)} async-done(((bf16[7168,128]{1,0:T(8,128)(2,1)}), bf16[896,128]{1,0:T(8,128)(2,1)}) %reduce-scatter.4.cloned.1.call-update) | async-done | bytes 229392
  609.2 1.8 copy.130
  (2092 shorter events, 450.1 us)
Async XLA Ops:
  6.5 516.1 %all-gather.2.cloned.1.call-start = ((), (), s32[]{:S(2)}) async-start(), calls=%async_computation.1 | async-start | bytes 15138816 | tf_op jit(solution)/shard_map/all_gather | solution.py:147
  7.3 602.0 %reduce-scatter.4.cloned.1.call-start = ((), (), s32[]{:S(2)}) async-start(), calls=%async_computation.2 | async-start | bytes 2064384
  31.5 16.3 %collective-permute-start = (bf16[128,576]{1,0:T(8,128)(2,1)S(1)}, bf16[128,576]{1,0:T(8,128)(2,1)S(1)}, u32[]{:S(2)}, u32[]{:S(2)}) collective-permute-start(bf16[128,576]{1,0:T(8,128)(2,1)S(1)} %copy.282), channel_id=1, source_target_pairs={{8,0},{16,8},{24,16},{32,24},{40,32},{48,40},{56,48},{64,56},{72,6... | collective-permute-start | bytes 442376 | tf_op jit(solution)/shard_map/while/body/eval_jaxpr/ppermute | solution.py:14
  47.9 16.0 %collective-permute-start = (bf16[128,576]{1,0:T(8,128)(2,1)S(1)}, bf16[128,576]{1,0:T(8,128)(2,1)S(1)}, u32[]{:S(2)}, u32[]{:S(2)}) collective-permute-start(bf16[128,576]{1,0:T(8,128)(2,1)S(1)} %copy.282), channel_id=1, source_target_pairs={{8,0},{16,8},{24,16},{32,24},{40,32},{48,40},{56,48},{64,56},{72,6... | collective-permute-start | bytes 442376 | tf_op jit(solution)/shard_map/while/body/eval_jaxpr/ppermute | solution.py:14
  63.9 16.0 %collective-permute-start = (bf16[128,576]{1,0:T(8,128)(2,1)S(1)}, bf16[128,576]{1,0:T(8,128)(2,1)S(1)}, u32[]{:S(2)}, u32[]{:S(2)}) collective-permute-start(bf16[128,576]{1,0:T(8,128)(2,1)S(1)} %copy.282), channel_id=1, source_target_pairs={{8,0},{16,8},{24,16},{32,24},{40,32},{48,40},{56,48},{64,56},{72,6... | collective-permute-start | bytes 442376 | tf_op jit(solution)/shard_map/while/body/eval_jaxpr/ppermute | solution.py:14
  79.9 16.0 %collective-permute-start = (bf16[128,576]{1,0:T(8,128)(2,1)S(1)}, bf16[128,576]{1,0:T(8,128)(2,1)S(1)}, u32[]{:S(2)}, u32[]{:S(2)}) collective-permute-start(bf16[128,576]{1,0:T(8,128)(2,1)S(1)} %copy.282), channel_id=1, source_target_pairs={{8,0},{16,8},{24,16},{32,24},{40,32},{48,40},{56,48},{64,56},{72,6... | collective-permute-start | bytes 442376 | tf_op jit(solution)/shard_map/while/body/eval_jaxpr/ppermute | solution.py:14
  96.0 16.0 %collective-permute-start = (bf16[128,576]{1,0:T(8,128)(2,1)S(1)}, bf16[128,576]{1,0:T(8,128)(2,1)S(1)}, u32[]{:S(2)}, u32[]{:S(2)}) collective-permute-start(bf16[128,576]{1,0:T(8,128)(2,1)S(1)} %copy.282), channel_id=1, source_target_pairs={{8,0},{16,8},{24,16},{32,24},{40,32},{48,40},{56,48},{64,56},{72,6... | collective-permute-start | bytes 442376 | tf_op jit(solution)/shard_map/while/body/eval_jaxpr/ppermute | solution.py:14
  112.1 16.0 %collective-permute-start = (bf16[128,576]{1,0:T(8,128)(2,1)S(1)}, bf16[128,576]{1,0:T(8,128)(2,1)S(1)}, u32[]{:S(2)}, u32[]{:S(2)}) collective-permute-start(bf16[128,576]{1,0:T(8,128)(2,1)S(1)} %copy.282), channel_id=1, source_target_pairs={{8,0},{16,8},{24,16},{32,24},{40,32},{48,40},{56,48},{64,56},{72,6... | collective-permute-start | bytes 442376 | tf_op jit(solution)/shard_map/while/body/eval_jaxpr/ppermute | solution.py:14
  128.1 16.0 %collective-permute-start = (bf16[128,576]{1,0:T(8,128)(2,1)S(1)}, bf16[128,576]{1,0:T(8,128)(2,1)S(1)}, u32[]{:S(2)}, u32[]{:S(2)}) collective-permute-start(bf16[128,576]{1,0:T(8,128)(2,1)S(1)} %copy.282), channel_id=1, source_target_pairs={{8,0},{16,8},{24,16},{32,24},{40,32},{48,40},{56,48},{64,56},{72,6... | collective-permute-start | bytes 442376 | tf_op jit(solution)/shard_map/while/body/eval_jaxpr/ppermute | solution.py:14
  144.1 16.0 %collective-permute-start = (bf16[128,576]{1,0:T(8,128)(2,1)S(1)}, bf16[128,576]{1,0:T(8,128)(2,1)S(1)}, u32[]{:S(2)}, u32[]{:S(2)}) collective-permute-start(bf16[128,576]{1,0:T(8,128)(2,1)S(1)} %copy.282), channel_id=1, source_target_pairs={{8,0},{16,8},{24,16},{32,24},{40,32},{48,40},{56,48},{64,56},{72,6... | collective-permute-start | bytes 442376 | tf_op jit(solution)/shard_map/while/body/eval_jaxpr/ppermute | solution.py:14
  160.1 16.0 %collective-permute-start = (bf16[128,576]{1,0:T(8,128)(2,1)S(1)}, bf16[128,576]{1,0:T(8,128)(2,1)S(1)}, u32[]{:S(2)}, u32[]{:S(2)}) collective-permute-start(bf16[128,576]{1,0:T(8,128)(2,1)S(1)} %copy.282), channel_id=1, source_target_pairs={{8,0},{16,8},{24,16},{32,24},{40,32},{48,40},{56,48},{64,56},{72,6... | collective-permute-start | bytes 442376 | tf_op jit(solution)/shard_map/while/body/eval_jaxpr/ppermute | solution.py:14
  176.1 16.0 %collective-permute-start = (bf16[128,576]{1,0:T(8,128)(2,1)S(1)}, bf16[128,576]{1,0:T(8,128)(2,1)S(1)}, u32[]{:S(2)}, u32[]{:S(2)}) collective-permute-start(bf16[128,576]{1,0:T(8,128)(2,1)S(1)} %copy.282), channel_id=1, source_target_pairs={{8,0},{16,8},{24,16},{32,24},{40,32},{48,40},{56,48},{64,56},{72,6... | collective-permute-start | bytes 442376 | tf_op jit(solution)/shard_map/while/body/eval_jaxpr/ppermute | solution.py:14
  192.1 16.0 %collective-permute-start = (bf16[128,576]{1,0:T(8,128)(2,1)S(1)}, bf16[128,576]{1,0:T(8,128)(2,1)S(1)}, u32[]{:S(2)}, u32[]{:S(2)}) collective-permute-start(bf16[128,576]{1,0:T(8,128)(2,1)S(1)} %copy.282), channel_id=1, source_target_pairs={{8,0},{16,8},{24,16},{32,24},{40,32},{48,40},{56,48},{64,56},{72,6... | collective-permute-start | bytes 442376 | tf_op jit(solution)/shard_map/while/body/eval_jaxpr/ppermute | solution.py:14
  208.2 16.0 %collective-permute-start = (bf16[128,576]{1,0:T(8,128)(2,1)S(1)}, bf16[128,576]{1,0:T(8,128)(2,1)S(1)}, u32[]{:S(2)}, u32[]{:S(2)}) collective-permute-start(bf16[128,576]{1,0:T(8,128)(2,1)S(1)} %copy.282), channel_id=1, source_target_pairs={{8,0},{16,8},{24,16},{32,24},{40,32},{48,40},{56,48},{64,56},{72,6... | collective-permute-start | bytes 442376 | tf_op jit(solution)/shard_map/while/body/eval_jaxpr/ppermute | solution.py:14
  224.2 16.0 %collective-permute-start = (bf16[128,576]{1,0:T(8,128)(2,1)S(1)}, bf16[128,576]{1,0:T(8,128)(2,1)S(1)}, u32[]{:S(2)}, u32[]{:S(2)}) collective-permute-start(bf16[128,576]{1,0:T(8,128)(2,1)S(1)} %copy.282), channel_id=1, source_target_pairs={{8,0},{16,8},{24,16},{32,24},{40,32},{48,40},{56,48},{64,56},{72,6... | collective-permute-start | bytes 442376 | tf_op jit(solution)/shard_map/while/body/eval_jaxpr/ppermute | solution.py:14
  240.2 16.0 %collective-permute-start = (bf16[128,576]{1,0:T(8,128)(2,1)S(1)}, bf16[128,576]{1,0:T(8,128)(2,1)S(1)}, u32[]{:S(2)}, u32[]{:S(2)}) collective-permute-start(bf16[128,576]{1,0:T(8,128)(2,1)S(1)} %copy.282), channel_id=1, source_target_pairs={{8,0},{16,8},{24,16},{32,24},{40,32},{48,40},{56,48},{64,56},{72,6... | collective-permute-start | bytes 442376 | tf_op jit(solution)/shard_map/while/body/eval_jaxpr/ppermute | solution.py:14
  256.2 16.0 %collective-permute-start = (bf16[128,576]{1,0:T(8,128)(2,1)S(1)}, bf16[128,576]{1,0:T(8,128)(2,1)S(1)}, u32[]{:S(2)}, u32[]{:S(2)}) collective-permute-start(bf16[128,576]{1,0:T(8,128)(2,1)S(1)} %copy.282), channel_id=1, source_target_pairs={{8,0},{16,8},{24,16},{32,24},{40,32},{48,40},{56,48},{64,56},{72,6... | collective-permute-start | bytes 442376 | tf_op jit(solution)/shard_map/while/body/eval_jaxpr/ppermute | solution.py:14
  272.2 16.0 %collective-permute-start = (bf16[128,576]{1,0:T(8,128)(2,1)S(1)}, bf16[128,576]{1,0:T(8,128)(2,1)S(1)}, u32[]{:S(2)}, u32[]{:S(2)}) collective-permute-start(bf16[128,576]{1,0:T(8,128)(2,1)S(1)} %copy.282), channel_id=1, source_target_pairs={{8,0},{16,8},{24,16},{32,24},{40,32},{48,40},{56,48},{64,56},{72,6... | collective-permute-start | bytes 442376 | tf_op jit(solution)/shard_map/while/body/eval_jaxpr/ppermute | solution.py:14
  288.2 16.0 %collective-permute-start = (bf16[128,576]{1,0:T(8,128)(2,1)S(1)}, bf16[128,576]{1,0:T(8,128)(2,1)S(1)}, u32[]{:S(2)}, u32[]{:S(2)}) collective-permute-start(bf16[128,576]{1,0:T(8,128)(2,1)S(1)} %copy.282), channel_id=1, source_target_pairs={{8,0},{16,8},{24,16},{32,24},{40,32},{48,40},{56,48},{64,56},{72,6... | collective-permute-start | bytes 442376 | tf_op jit(solution)/shard_map/while/body/eval_jaxpr/ppermute | solution.py:14
  304.3 16.0 %collective-permute-start = (bf16[128,576]{1,0:T(8,128)(2,1)S(1)}, bf16[128,576]{1,0:T(8,128)(2,1)S(1)}, u32[]{:S(2)}, u32[]{:S(2)}) collective-permute-start(bf16[128,576]{1,0:T(8,128)(2,1)S(1)} %copy.282), channel_id=1, source_target_pairs={{8,0},{16,8},{24,16},{32,24},{40,32},{48,40},{56,48},{64,56},{72,6... | collective-permute-start | bytes 442376 | tf_op jit(solution)/shard_map/while/body/eval_jaxpr/ppermute | solution.py:14
  320.3 16.0 %collective-permute-start = (bf16[128,576]{1,0:T(8,128)(2,1)S(1)}, bf16[128,576]{1,0:T(8,128)(2,1)S(1)}, u32[]{:S(2)}, u32[]{:S(2)}) collective-permute-start(bf16[128,576]{1,0:T(8,128)(2,1)S(1)} %copy.282), channel_id=1, source_target_pairs={{8,0},{16,8},{24,16},{32,24},{40,32},{48,40},{56,48},{64,56},{72,6... | collective-permute-start | bytes 442376 | tf_op jit(solution)/shard_map/while/body/eval_jaxpr/ppermute | solution.py:14
  336.3 16.0 %collective-permute-start = (bf16[128,576]{1,0:T(8,128)(2,1)S(1)}, bf16[128,576]{1,0:T(8,128)(2,1)S(1)}, u32[]{:S(2)}, u32[]{:S(2)}) collective-permute-start(bf16[128,576]{1,0:T(8,128)(2,1)S(1)} %copy.282), channel_id=1, source_target_pairs={{8,0},{16,8},{24,16},{32,24},{40,32},{48,40},{56,48},{64,56},{72,6... | collective-permute-start | bytes 442376 | tf_op jit(solution)/shard_map/while/body/eval_jaxpr/ppermute | solution.py:14
  352.3 16.0 %collective-permute-start = (bf16[128,576]{1,0:T(8,128)(2,1)S(1)}, bf16[128,576]{1,0:T(8,128)(2,1)S(1)}, u32[]{:S(2)}, u32[]{:S(2)}) collective-permute-start(bf16[128,576]{1,0:T(8,128)(2,1)S(1)} %copy.282), channel_id=1, source_target_pairs={{8,0},{16,8},{24,16},{32,24},{40,32},{48,40},{56,48},{64,56},{72,6... | collective-permute-start | bytes 442376 | tf_op jit(solution)/shard_map/while/body/eval_jaxpr/ppermute | solution.py:14
  368.3 16.0 %collective-permute-start = (bf16[128,576]{1,0:T(8,128)(2,1)S(1)}, bf16[128,576]{1,0:T(8,128)(2,1)S(1)}, u32[]{:S(2)}, u32[]{:S(2)}) collective-permute-start(bf16[128,576]{1,0:T(8,128)(2,1)S(1)} %copy.282), channel_id=1, source_target_pairs={{8,0},{16,8},{24,16},{32,24},{40,32},{48,40},{56,48},{64,56},{72,6... | collective-permute-start | bytes 442376 | tf_op jit(solution)/shard_map/while/body/eval_jaxpr/ppermute | solution.py:14
  384.3 16.0 %collective-permute-start = (bf16[128,576]{1,0:T(8,128)(2,1)S(1)}, bf16[128,576]{1,0:T(8,128)(2,1)S(1)}, u32[]{:S(2)}, u32[]{:S(2)}) collective-permute-start(bf16[128,576]{1,0:T(8,128)(2,1)S(1)} %copy.282), channel_id=1, source_target_pairs={{8,0},{16,8},{24,16},{32,24},{40,32},{48,40},{56,48},{64,56},{72,6... | collective-permute-start | bytes 442376 | tf_op jit(solution)/shard_map/while/body/eval_jaxpr/ppermute | solution.py:14
  400.4 16.0 %collective-permute-start = (bf16[128,576]{1,0:T(8,128)(2,1)S(1)}, bf16[128,576]{1,0:T(8,128)(2,1)S(1)}, u32[]{:S(2)}, u32[]{:S(2)}) collective-permute-start(bf16[128,576]{1,0:T(8,128)(2,1)S(1)} %copy.282), channel_id=1, source_target_pairs={{8,0},{16,8},{24,16},{32,24},{40,32},{48,40},{56,48},{64,56},{72,6... | collective-permute-start | bytes 442376 | tf_op jit(solution)/shard_map/while/body/eval_jaxpr/ppermute | solution.py:14
  416.4 16.0 %collective-permute-start = (bf16[128,576]{1,0:T(8,128)(2,1)S(1)}, bf16[128,576]{1,0:T(8,128)(2,1)S(1)}, u32[]{:S(2)}, u32[]{:S(2)}) collective-permute-start(bf16[128,576]{1,0:T(8,128)(2,1)S(1)} %copy.282), channel_id=1, source_target_pairs={{8,0},{16,8},{24,16},{32,24},{40,32},{48,40},{56,48},{64,56},{72,6... | collective-permute-start | bytes 442376 | tf_op jit(solution)/shard_map/while/body/eval_jaxpr/ppermute | solution.py:14
  432.4 16.0 %collective-permute-start = (bf16[128,576]{1,0:T(8,128)(2,1)S(1)}, bf16[128,576]{1,0:T(8,128)(2,1)S(1)}, u32[]{:S(2)}, u32[]{:S(2)}) collective-permute-start(bf16[128,576]{1,0:T(8,128)(2,1)S(1)} %copy.282), channel_id=1, source_target_pairs={{8,0},{16,8},{24,16},{32,24},{40,32},{48,40},{56,48},{64,56},{72,6... | collective-permute-start | bytes 442376 | tf_op jit(solution)/shard_map/while/body/eval_jaxpr/ppermute | solution.py:14
  448.4 16.0 %collective-permute-start = (bf16[128,576]{1,0:T(8,128)(2,1)S(1)}, bf16[128,576]{1,0:T(8,128)(2,1)S(1)}, u32[]{:S(2)}, u32[]{:S(2)}) collective-permute-start(bf16[128,576]{1,0:T(8,128)(2,1)S(1)} %copy.282), channel_id=1, source_target_pairs={{8,0},{16,8},{24,16},{32,24},{40,32},{48,40},{56,48},{64,56},{72,6... | collective-permute-start | bytes 442376 | tf_op jit(solution)/shard_map/while/body/eval_jaxpr/ppermute | solution.py:14
  464.4 16.0 %collective-permute-start = (bf16[128,576]{1,0:T(8,128)(2,1)S(1)}, bf16[128,576]{1,0:T(8,128)(2,1)S(1)}, u32[]{:S(2)}, u32[]{:S(2)}) collective-permute-start(bf16[128,576]{1,0:T(8,128)(2,1)S(1)} %copy.282), channel_id=1, source_target_pairs={{8,0},{16,8},{24,16},{32,24},{40,32},{48,40},{56,48},{64,56},{72,6... | collective-permute-start | bytes 442376 | tf_op jit(solution)/shard_map/while/body/eval_jaxpr/ppermute | solution.py:14
  480.4 16.0 %collective-permute-start = (bf16[128,576]{1,0:T(8,128)(2,1)S(1)}, bf16[128,576]{1,0:T(8,128)(2,1)S(1)}, u32[]{:S(2)}, u32[]{:S(2)}) collective-permute-start(bf16[128,576]{1,0:T(8,128)(2,1)S(1)} %copy.282), channel_id=1, source_target_pairs={{8,0},{16,8},{24,16},{32,24},{40,32},{48,40},{56,48},{64,56},{72,6... | collective-permute-start | bytes 442376 | tf_op jit(solution)/shard_map/while/body/eval_jaxpr/ppermute | solution.py:14
  496.5 16.0 %collective-permute-start = (bf16[128,576]{1,0:T(8,128)(2,1)S(1)}, bf16[128,576]{1,0:T(8,128)(2,1)S(1)}, u32[]{:S(2)}, u32[]{:S(2)}) collective-permute-start(bf16[128,576]{1,0:T(8,128)(2,1)S(1)} %copy.282), channel_id=1, source_target_pairs={{8,0},{16,8},{24,16},{32,24},{40,32},{48,40},{56,48},{64,56},{72,6... | collective-permute-start | bytes 442376 | tf_op jit(solution)/shard_map/while/body/eval_jaxpr/ppermute | solution.py:14
  (1 other events, 15.4 us)
Sparse Core Ops, SparseCore 0:
  9.2 98.3 all-gather.1
  535.3 73.8 reduce-scatter.3
where the time goes:
time: 629 us; the launch traced here: 618 us
  matrix products  201 us (32%)
  loops' own time  175 us (28%)
  local copies, waits for them, and re-layouts  124 us (20%)
  waiting for transfers between devices  74.9 us (12%)
  other arithmetic  20.2 us (3%)
  between operations  18.8 us (3%)
    another operation x1, loops' own time, on_device(): lax.fori_loop(0, cycle_size - 1, pass_turn, (latent_block, softmax_state))  164 us
    unnamed x3, waiting for transfers between devices  74.8 us
    dot_general x32, matrix products, attend_block(): jnp.dot(latent, w_uv, preferred_element_type=jnp.float32)  49.3 us
    dot_general x32, matrix products, attend_block(): jnp.dot(latent, w_uk, preferred_element_type=jnp.float32)  49.1 us
    slice x63, local copies, waits for them, and re-layouts, attend_block(): visible_any = key_pos[key_start] <= query_pos[row_stop - 1]  41.7 us
    dot_general x127, matrix products, attend_quarter(): jnp.einsum('qhk,khd->qhd', probabilities.astype(jnp.bfloat16), values, pr...  35.9 us
    dot_general x127, matrix products, attend_quarter(): jnp.einsum('qhd,kd->qhk', shaped[:, :, NOPE:], keys_rotary, preferred_ele...  33.8 us
    slice x32, local copies, waits for them, and re-layouts, attend_block(): query_rows[row_start:row_stop]  33.7 us
  transfers between devices with their start and end apart: 33, of which 1 were waited for; matrix products, arithmetic and copies ran while one was open for 54% of the time, Pallas kernels for 0%

commit v1 on v0

v1 whole, which is shorter than its diff:
```python
import functools
import math

import jax
import jax.numpy as jnp
from jax import lax
from jax.experimental import pallas as pl
from jax.experimental.pallas import tpu as pltpu
from jax.sharding import PartitionSpec as P

LATENT = 512
ROPE = 64
NOPE = 128
HD = NOPE + ROPE
SCALE = HD ** -0.5 * math.log2(math.e)
NT = (((1,), (1,)), ((), ()))


def attention_kernel(q_ref, lat_ref, uk_ref, uv_ref, out_ref, qc_ref, qr_ref, m_ref, l_ref, acc_ref):
    rows = q_ref.shape[0]
    heads = uk_ref.shape[1] // NOPE
    total = rows * heads
    block = 512
    chunk = 256
    me = lax.axis_index("ctx")
    first = me * rows
    z = first // block
    for h in range(heads):
        qh = q_ref[:, h * HD:h * HD + NOPE]
        qa = lax.dot_general(qh, uk_ref[:, h * NOPE:(h + 1) * NOPE], NT, preferred_element_type=jnp.float32)
        qc_ref[h * rows:(h + 1) * rows, :] = (qa * SCALE).astype(jnp.bfloat16)
        qr = q_ref[:, h * HD + NOPE:(h + 1) * HD].astype(jnp.float32)
        qr_ref[h * rows:(h + 1) * rows, :] = (qr * SCALE).astype(jnp.bfloat16)

    def visit(at, masked):
        start = pl.multiple_of(at * block, block)
        lat = lat_ref[pl.ds(start, block), :LATENT]
        rot = lat_ref[pl.ds(start, block), LATENT:]
        for r in range(0, total, chunk):
            s = lax.dot_general(qc_ref[r:r + chunk, :], lat, NT, preferred_element_type=jnp.float32)
            s = s + lax.dot_general(qr_ref[r:r + chunk, :], rot, NT, preferred_element_type=jnp.float32)
            if masked:
                row = first - start + lax.rem(lax.broadcasted_iota(jnp.int32, s.shape, 0), rows)
                s = jnp.where(row >= lax.broadcasted_iota(jnp.int32, s.shape, 1), s, -jnp.inf)
                m_new = jnp.max(s, axis=1, keepdims=True)
                p = jnp.exp2(s - m_new)
                l_ref[r:r + chunk, :] = jnp.sum(p, axis=1, keepdims=True)
                acc_ref[r:r + chunk, :] = jnp.dot(p.astype(jnp.bfloat16), lat, preferred_element_type=jnp.float32)
            else:
                m_old = m_ref[r:r + chunk, :]
                m_new = jnp.maximum(m_old, jnp.max(s, axis=1, keepdims=True))
                alpha = jnp.exp2(m_old - m_new)
                p = jnp.exp2(s - m_new)
                l_ref[r:r + chunk, :] = l_ref[r:r + chunk, :] * alpha + jnp.sum(p, axis=1, keepdims=True)
                acc_ref[r:r + chunk, :] = acc_ref[r:r + chunk, :] * alpha + jnp.dot(
                    p.astype(jnp.bfloat16), lat, preferred_element_type=jnp.float32)
            m_ref[r:r + chunk, :] = m_new

    visit(z, True)

    @pl.loop(0, z)
    def _(at):
        visit(at, False)

    for h in range(heads):
        o = acc_ref[h * rows:(h + 1) * rows, :] / l_ref[h * rows:(h + 1) * rows, :]
        a = jnp.dot(o.astype(jnp.bfloat16), uv_ref[:, h * NOPE:(h + 1) * NOPE], preferred_element_type=jnp.float32)
        out_ref[:, h * NOPE:(h + 1) * NOPE] = a.astype(jnp.bfloat16)


def compress_norm(compressed, latent_gain):
    latent = compressed[:, :LATENT].astype(jnp.float32)
    mean_square = jnp.mean(latent * latent, axis=1, keepdims=True)
    normed = (latent * lax.rsqrt(mean_square + 1e-06) * latent_gain).astype(jnp.bfloat16)
    return jnp.concatenate([normed, compressed[:, LATENT:]], axis=1)


def on_device(queries, compressed, latent_gain, w_uk, w_uv, w_out):
    rows = queries.shape[0]
    heads = w_uk.shape[1] // NOPE
    ctx = lax.axis_size("ctx")
    along_z = [[j + 4 * z for z in range(ctx // 4)] for j in range(4)]
    within = [[4 * z + j for j in range(4)] for z in range(ctx // 4)]
    latents = lax.all_gather(compress_norm(compressed, latent_gain), "ctx", axis=0, tiled=True)
    w_all = lax.all_gather(w_out, "ctx", axis=0, tiled=False, axis_index_groups=along_z)
    attention = pl.pallas_call(
        attention_kernel,
        out_shape=jax.ShapeDtypeStruct((rows, heads * NOPE), jnp.bfloat16),
        in_specs=[pl.BlockSpec(memory_space=pltpu.VMEM)] * 4,
        out_specs=pl.BlockSpec(memory_space=pltpu.VMEM),
        scratch_shapes=[
            pltpu.VMEM((rows * heads, LATENT), jnp.bfloat16),
            pltpu.VMEM((rows * heads, ROPE), jnp.bfloat16),
            pltpu.VMEM((rows * heads, 1), jnp.float32),
            pltpu.VMEM((rows * heads, 1), jnp.float32),
            pltpu.VMEM((rows * heads, LATENT), jnp.float32),
        ],
        compiler_params=pltpu.CompilerParams(vmem_limit_bytes=48 * 1024 * 1024),
        name="attention",
    )(queries, latents, w_uk, w_uv)
    strip = lax.all_gather(attention, "ctx", axis=0, tiled=True, axis_index_groups=within)
    partial = jnp.einsum("tk,zkn->ztn", strip, w_all, preferred_element_type=jnp.float32).astype(jnp.bfloat16)
    mine = lax.psum_scatter(partial, "head", scatter_dimension=0, tiled=False)
    mine = mine.reshape(4, rows, mine.shape[1])
    swapped = lax.all_to_all(mine, "ctx", 0, 0, axis_index_groups=within, tiled=True)
    return jnp.transpose(swapped, (1, 0, 2)).reshape(rows, -1)


def solution(mesh):
    return jax.shard_map(
        on_device,
        mesh=mesh,
        in_specs=(
            P("ctx", "head"),
            P("ctx", None),
            P(),
            P(None, "head"),
            P(None, "head"),
            P("head", "ctx"),
        ),
        out_specs=P("ctx", "head"),
        check_vma=False,
    )
```

time: 629 us -> 260 us (0.41)
  the two profiles are of different devices: /device:TPU:239 before, /device:TPU:1 now
where the time goes in v1:
time: 260 us
  waiting for transfers between devices  212 us (82%)
  between operations  13.2 us (5%)
  local copies, waits for them, and re-layouts  11.5 us (4%)
  blocking collectives  9.26 us (4%)
  Pallas kernels  6.25 us (2%)
  matrix products  4.58 us (2%)
  other arithmetic  3.07 us (1%)
    reduce_scatter x1, waiting for transfers between devices, on_device(): mine = lax.psum_scatter(partial, 'head', scatter_dimension=0, tiled=False)  78.3 us
    all_gather x1, waiting for transfers between devices, on_device(): lax.all_gather(compress_norm(compressed, latent_gain), 'ctx', axis=0, til...  71.8 us
    all_gather x1, waiting for transfers between devices, on_device(): lax.all_gather(w_out, 'ctx', axis=0, tiled=False, axis_index_groups=along_z)  41.4 us
    all_gather x1, waiting for transfers between devices, on_device(): lax.all_gather(attention, 'ctx', axis=0, tiled=True, axis_index_groups=wi...  19.7 us
    all_to_all x1, blocking collectives, on_device(): lax.all_to_all(mine, 'ctx', 0, 0, axis_index_groups=within, tiled=True)  9.26 us
    pallas_call x1, Pallas kernels, on_device(): pl.pallas_call(attention_kernel, out_shape=jax.ShapeDtypeStruct((rows, he...  6.25 us
  transfers between devices with their start and end apart: 4, of which 4 were waited for; matrix products, arithmetic and copies ran while one was open for 2% of the time, Pallas kernels for 2%

profile of v1, /device:TPU:1, one launch (start us, length us, event | category | flops | bytes accessed | tf_op | source)
XLA Modules:
  0.0 259.9 jit_solution(12385093044003207994)
XLA Ops:
  6.5 0.0 all-gather.5.cloned.1.call-start
  6.5 0.9 slice.6
  7.5 0.7 slice.7
  8.2 0.1 copy.15
  8.3 0.1 fusion
  8.4 0.1 copy.16
  8.5 0.8 fusion.2
  9.3 0.7 pad_maximum_fusion
  10.0 0.0 all-gather.5.cloned.1.call-update
  10.0 0.0 all-gather.9.cloned.1.call-start
  10.1 0.7 all-gather.9.cloned.1.call-update
  10.8 0.0 all-gather.7.cloned.1.call-start
  10.8 71.8 %all-gather.5.cloned.1.call-done.lat_ref = bf16[4096,576]{1,0:T(8,128)(2,1)} async-done(((bf16[128,576]{1,0:T(8,128)(2,1)}), bf16[4096,576]{1,0:T(8,128)(2,1)}) %all-gather.5.cloned.1.call-update) | async-done | bytes 4718608 | tf_op jit(solution)/shard_map/all_gather | solution.py:84
  82.6 0.0 copy-start
  82.6 1.2 copy-done
  83.8 0.0 copy-start.1
  83.8 1.2 copy-done.1
  85.1 0.0 copy-start.2
  85.1 1.0 copy-done.2
  86.1 6.2 %attention.1 = bf16[128,1024]{1,0:T(8,128)(2,1)} custom-call(bf16[128,1536]{1,0:T(8,128)(2,1)S(1)} %copy-done.2, bf16[4096,576]{1,0:T(8,128)(2,1)} %all-gather.5.cloned.1.call-done.lat_ref, bf16[512,1024]{1,0:T(8,128)(2,1)S(1)} %copy-done, bf16[512,1024]{1,0:T(8,128)(2,1)S(1)} %copy-done.1), custom_call_target="tpu_custom_call" | custom-call | tf_op jit(solution)/shard_map/attention/pallas_call | solution.py:86
  92.3 0.0 all-gather.7.cloned.1.call-update
  92.3 0.0 reduce-scatter.2.cloned.1.call-start
  92.4 41.4 %all-gather.9.cloned.1.call-done = bf16[8192,224]{0,1:T(8,128)(2,1)} async-done(((bf16[1024,224]{0,1:T(8,128)(2,1)}), bf16[8192,224]{0,1:T(8,128)(2,1)}) %all-gather.9.cloned.1.call-update) | async-done | bytes 3670032 | tf_op jit(solution)/shard_map/all_gather | solution.py:85
  133.7 4.4 %copy.19 = bf16[28,8,8,1024]{3,2,0,1:T(8,128)(2,1)} copy(bf16[28,8,8,1024]{3,2,1,0:T(8,128)(2,1)} %bitcast.17) | data formatting | bytes 7340032 | tf_op jit(solution)/shard_map/all_gather | solution.py:85
  138.1 19.7 %all-gather.7.cloned.1.call-done = bf16[512,1024]{1,0:T(8,128)(2,1)} async-done(((bf16[128,1024]{1,0:T(8,128)(2,1)}), bf16[512,1024]{1,0:T(8,128)(2,1)}) %all-gather.7.cloned.1.call-update) | async-done | bytes 1048592 | tf_op jit(solution)/shard_map/all_gather | solution.py:101
  157.8 4.6 %fusion.3 = f32[512,1792]{0,1:S(1)} fusion(bf16[512,1024]{1,0:T(8,128)(2,1)} %all-gather.7.cloned.1.call-done, bf16[1024,1792]{0,1:T(8,128)(2,1)} %bitcast.18), kind=kOutput, calls=%fused_computation.9 | convolution fusion | flops 1879048192 | bytes 8388608
  162.4 1.5 convert_bitcast_fusion
  163.9 0.0 reduce-scatter.2.cloned.1.call-update
  163.9 78.3 %reduce-scatter.2.cloned.1.call-done = bf16[1,512,224]{1,2,0:T(8,128)(2,1)} async-done(((bf16[8,512,224]{1,2,0:T(8,128)(2,1)}), bf16[1,512,224]{1,2,0:T(8,128)(2,1)}) %reduce-scatter.2.cloned.1.call-update) | async-done | bytes 229392 | tf_op jit(solution)/shard_map/reduce_scatter | solution.py:103
  242.2 1.0 reshape_reduce_scatter.3
  243.2 9.3 %all_to_all.5 = bf16[4,128,224]{1,2,0:T(8,128)(2,1)S(1)} all-to-all(bf16[4,128,224]{1,2,0:T(8,128)(2,1)S(1)} %copy.13), channel_id=1, replica_groups={{0,8,16,24},{32,40,48,56},{64,72,80,88},{96,104,112,120},{128,136,144,1..., dimensions={0} | all-to-all | bytes 458752 | tf_op jit(solution)/shard_map/all_to_all | solution.py:105
  252.5 0.8 copy.14
  (2 shorter events, 0.0 us)
Async XLA Ops:
  6.5 76.1 %all-gather.5.cloned.1.call-start = ((), (), s32[]{:S(2)}) async-start(), calls=%async_computation.2 | async-start | bytes 5406720 | tf_op jit(solution)/shard_map/all_gather | solution.py:84
  10.0 123.7 %all-gather.9.cloned.1.call-start = ((), (), s32[]{:S(2)}) async-start(), calls=%async_computation.5 | async-start | bytes 4128768 | tf_op jit(solution)/shard_map/all_gather | solution.py:85
  10.8 147.0 %all-gather.7.cloned.1.call-start = ((), (), s32[]{:S(2)}) async-start(), calls=%async_computation.3 | async-start | bytes 1310720 | tf_op jit(solution)/shard_map/all_gather | solution.py:101
  82.6 1.2 copy-start
  83.8 1.2 copy-start.1
  85.1 1.0 copy-start.2
  92.3 149.9 %reduce-scatter.2.cloned.1.call-start = ((), (), s32[]{:S(2)}) async-start(), calls=%async_computation.4 | async-start | bytes 2064384 | tf_op jit(solution)/shard_map/reduce_scatter | solution.py:103
Sparse Core Ops, SparseCore 0:
  10.2 72.3 all-gather.4
  84.4 49.2 all-gather.8
  135.5 22.2 all-gather.6
  164.1 78.0 reduce-scatter.1

commit v2 on v1

v2 whole, which is shorter than its diff:
```python
import math

import jax
import jax.numpy as jnp
from jax import lax
from jax.experimental import pallas as pl
from jax.experimental.pallas import tpu as pltpu
from jax.sharding import PartitionSpec as P

LATENT = 512
ROPE = 64
NOPE = 128
HD = NOPE + ROPE
WIDE = 640
ROWS = 128
HEADS = 8
STRIP = 4 * ROWS
TOTAL = HEADS * ROWS
CHUNK = 512
HALF = 112
NZ = 8
SCALE = HD ** -0.5 * math.log2(math.e)
NT = (((1,), (1,)), ((), ()))
MESH = pl.DeviceIdType.MESH


def al(value, unit):
    return pl.multiple_of(value, unit)


def kernel(q_ref, comp_ref, gain_ref, uk_ref, uv_ref, w_ref, out_ref,
           lat, ball, qt, uvt, m_ref, l_ref, acc, abuf, cbuf, rbuf, fsrc, fin,
           s1s, s1r, s2s, s2r, s3s, s3r, s4s, s4r, brs, brr, bls, blr,
           axs, axr, acs, acr, afs, afr, cs, cr, fs, fr):
    ctx = lax.axis_index("ctx")
    head = lax.axis_index("head")
    z = ctx // 4
    j = ctx % 4
    y = head // 2
    xh = head % 2
    xl = j // 2
    base = 4 * z
    sib = j + 1 - 2 * (j % 2)
    opp = (j + 2) % 4
    opp_sib = (sib + 2) % 4
    x_lo = (base + opp, head)
    core = (base + sib, head)
    x_up = (base + opp, 2 * y + (xh + xl) % 2)
    x_down = (base + opp, 2 * y + (xh + xl + 1) % 2)
    z_up = (4 * ((z + 1) % NZ) + j, head)
    z_down = (4 * ((z + 7) % NZ) + j, head)

    def copy(src, dst, send, recv, device):
        return pltpu.make_async_remote_copy(
            src_ref=src, dst_ref=dst, send_sem=send, recv_sem=recv, device_id=device, device_id_type=MESH)

    def arrived(dst, recv):
        copy(dst, dst, recv, recv, core).wait_recv()

    def left(src, send):
        copy(src, src, send, send, core).wait_send()

    barrier = pltpu.get_barrier_semaphore()

    def greet(device):
        pl.semaphore_signal(barrier, inc=1, device_id=device, device_id_type=MESH)

    for k in range(1, NZ):
        greet((4 * ((z + k) % NZ) + j, head))
    for k in range(1, HEADS):
        greet((ctx, (head + k) % HEADS))
    greet(x_up)
    greet(x_down)
    greet(core)
    for p in range(4):
        for b in range(2):
            @pl.when((p != j) | (j != y) | (b != xh))
            def _():
                greet((base + p, 2 * j + b))

    own = comp_ref[:, :LATENT].astype(jnp.float32)
    mean_square = jnp.mean(own * own, axis=1, keepdims=True)
    normed = (own * lax.rsqrt(mean_square + 1e-06) * gain_ref[...]).astype(jnp.bfloat16)
    mine = pl.ds(al(j * ROWS, ROWS), ROWS)
    lat[z, mine, :LATENT] = normed
    lat[z, mine, LATENT:] = jnp.concatenate(
        [comp_ref[:, LATENT:], jnp.zeros((ROWS, WIDE - LATENT - ROPE), jnp.bfloat16)], axis=1)
    wt = w_ref[...].T
    ball[z, 0] = wt[:HALF]
    ball[z, 1] = wt[HALF:]

    pl.semaphore_wait(barrier, jnp.where(j == y, 24, 25))

    def rows_of(zs, member, start, count):
        return lat.at[zs, pl.ds(al(member * ROWS + start, 16), count), :]

    def z_copy(k):
        part = rows_of(z, j, y * 32, 32)
        return copy(part, part, s1s.at[k], s1r.at[z], (4 * (z + k) + j, head))

    for k in range(1, NZ):
        @pl.when(z + k < NZ)
        def _():
            z_copy(k).start()

    def y_copy(zs, k):
        part = rows_of(zs, j, y * 32, 32)
        return copy(part, part, s2s.at[zs, k - 1], s2r.at[zs, k - 1], (ctx, 2 * ((y + k) % 4) + xh))

    def x_copies(zs):
        low = rows_of(zs, j, 0, 64)
        high = rows_of(zs, j, 64, 64)
        return (copy(low, low, s3s.at[zs, 0], s3r.at[zs, 0], x_up),
                copy(high, high, s3s.at[zs, 1], s3r.at[zs, 1], x_down))

    def core_copy(zs, member, slot):
        part = rows_of(zs, member, 0, ROWS)
        return copy(part, part, s4s.at[zs, slot], s4r.at[zs, slot], core)

    def stage1(d):
        zs = z - d
        arrived(rows_of(zs, j, y * 32, 32), s1r.at[zs])
        for k in range(1, 4):
            y_copy(zs, k).start()

    def stage2(d, wait=True):
        zs = z - d
        if wait:
            for k in range(1, 4):
                arrived(rows_of(zs, j, ((y + 4 - k) % 4) * 32, 32), s2r.at[zs, k - 1])
        for each in x_copies(zs):
            each.start()
        core_copy(zs, j, 0).start()

    def stage3(d):
        zs = z - d
        arrived(rows_of(zs, opp, 0, 64), s3r.at[zs, 0])
        arrived(rows_of(zs, opp, 64, 64), s3r.at[zs, 1])
        core_copy(zs, opp, 1).start()

    def stage4(d):
        zs = z - d
        arrived(rows_of(zs, sib, 0, ROWS), s4r.at[zs, 0])
        arrived(rows_of(zs, opp_sib, 0, ROWS), s4r.at[zs, 1])

    def ring_up(u):
        part = ball.at[(z + NZ - u // 2) % NZ, u % 2]
        return copy(part, part, brs.at[u], brr.at[u], z_up)

    def ring_down(u):
        part = ball.at[(z + u // 2) % NZ, 1 - u % 2]
        return copy(part, part, bls.at[u], blr.at[u], z_down)

    def ring_arrived(k):
        arrived(ball.at[(z + 7 - k // 2) % NZ, k % 2], brr.at[k])
        arrived(ball.at[(z + 1 + k // 2) % NZ, 1 - k % 2], blr.at[k])

    def forward(k):
        ring_arrived(k)

        @pl.when(k < 5)
        def _():
            ring_up(k + 2).start()
            ring_down(k + 2).start()

    def when_in(d, act):
        @pl.when(d <= z)
        def _():
            act(d)

    stage2(0, wait=False)
    for u in range(2):
        ring_up(u).start()
        ring_down(u).start()

    def absorb(h):
        lanes = slice(h * ROWS, (h + 1) * ROWS)
        qa = lax.dot_general(uk_ref[:, h * NOPE:(h + 1) * NOPE], q_ref[:, h * HD:h * HD + NOPE], NT,
                             preferred_element_type=jnp.float32)
        qt[:LATENT, lanes] = (qa * SCALE).astype(jnp.bfloat16)
        qr = q_ref[:, h * HD + NOPE:(h + 1) * HD].astype(jnp.float32) * SCALE
        qt[LATENT:LATENT + ROPE, lanes] = qr.T.astype(jnp.bfloat16)

    qt[LATENT + ROPE:, :] = jnp.zeros((WIDE - LATENT - ROPE, TOTAL), jnp.bfloat16)
    for h in range(HEADS):
        absorb(h)
    when_in(1, stage1)
    when_in(2, stage1)
    uvt[...] = uv_ref[...].T

    def visit(zs, first):
        block = lat[zs]
        turned = block[:, :LATENT].T

        def score(c):
            s = jnp.dot(block, qt[:, c * CHUNK:(c + 1) * CHUNK], preferred_element_type=jnp.float32)
            if first:
                row = j * ROWS + lax.broadcasted_iota(jnp.int32, s.shape, 1) % ROWS
                s = jnp.where(row >= lax.broadcasted_iota(jnp.int32, s.shape, 0), s, -jnp.inf)
            return s

        def rest(s, c):
            lanes = slice(c * CHUNK, (c + 1) * CHUNK)
            m_new = jnp.max(s, axis=0, keepdims=True)
            if not first:
                m_old = m_ref[:, lanes]
                m_new = jnp.maximum(m_old, m_new)
                alpha = jnp.exp2(m_old - m_new)
            p = jnp.exp2(s - m_new)
            total = jnp.sum(p, axis=0, keepdims=True)
            part = jnp.dot(turned, p.astype(jnp.bfloat16), preferred_element_type=jnp.float32)
            m_ref[:, lanes] = m_new
            if first:
                l_ref[:, lanes] = total
                acc[:, lanes] = part
            else:
                l_ref[:, lanes] = l_ref[:, lanes] * alpha + total
                acc[:, lanes] = acc[:, lanes] * alpha + part

        s = score(0)
        later = score(1)
        rest(s, 0)
        rest(later, 1)

    when_in(1, stage2)
    stage3(0)
    when_in(3, stage1)
    when_in(2, stage2)
    when_in(1, stage3)
    stage4(0)
    visit(z, True)

    @pl.loop(1, z + 1)
    def _(i):
        when_in(i + 3, stage1)
        when_in(i + 2, stage2)
        when_in(i + 1, stage3)
        stage4(i)
        visit(z - i, False)

        @pl.when(i % 2 == 0)
        def _():
            forward(i // 2 - 1)

    done = z // 2

    def piece(member, c):
        return abuf.at[pl.ds(c * CHUNK, CHUNK), pl.ds(al(member * ROWS, ROWS), ROWS)]

    def a_x(c):
        return copy(piece(j, c), piece(j, c), axs.at[c], axr.at[c], x_lo)

    def a_core(c):
        return copy(piece(j, c), piece(j, c), acs.at[c], acr.at[c], core)

    def a_forward(c):
        return copy(piece(opp, c), piece(opp, c), afs.at[c], afr.at[c], core)

    for c in range(2):
        for h in range(c * 4, c * 4 + 4):
            lanes = slice(h * ROWS, (h + 1) * ROWS)
            o = (acc[:, lanes] / l_ref[:, lanes]).astype(jnp.bfloat16)
            a = jnp.dot(uvt[h * NOPE:(h + 1) * NOPE, :], o, preferred_element_type=jnp.float32)
            abuf[h * NOPE:(h + 1) * NOPE, mine] = a.astype(jnp.bfloat16)
        a_x(c).start()
        a_core(c).start()
    for c in range(2):
        arrived(piece(opp, c), axr.at[c])
        a_forward(c).start()
    for c in range(2):
        arrived(piece(sib, c), acr.at[c])
    for c in range(2):
        arrived(piece(opp_sib, c), afr.at[c])

    def places(s):
        u = jnp.maximum(s - 1, 0)
        far = (s + 1) // 2
        up = (z + NZ - far) % NZ
        down = (z + far) % NZ
        return up, down, u % 2

    def c_copy(s, r, t, b):
        return copy(cbuf.at[s, r, t], rbuf.at[s, head], cs.at[s, r, t], cr.at[s, head], (ctx, 2 * t + b))

    def each_copy(s, act):
        odd = places(s)[2]
        for r in range(2):
            b = (odd + r) % 2
            for t in range(4):
                @pl.when((t != y) | (b != xh))
                def _():
                    act(c_copy(s, r, t, b))

    def multiply(s):
        up, down, odd = places(s)
        both = jnp.concatenate([ball[up, odd], ball[down, 1 - odd]], axis=0)
        ct = jnp.dot(both, abuf[...], preferred_element_type=jnp.float32).astype(jnp.bfloat16)
        for r in range(2):
            for t in range(4):
                cbuf[s, r, t] = ct[r * HALF:(r + 1) * HALF, t * ROWS:(t + 1) * ROWS]
        each_copy(s, lambda each: each.start())

    def home(s):
        up, down, odd = places(s)
        same = (odd + xh) % 2
        return up * (1 - same) + down * same, same

    spot = fin.at[pl.ds(al((2 * j + xh) * HALF, HALF), HALF), :]

    def f_copy(s):
        n, _ = home(s)
        return copy(fsrc.at[s], spot, fs.at[s], fr.at[2 * j + xh], (base + y, n))

    def is_here(s):
        return (y == j) & (home(s)[0] == head)

    def gather(s):
        n, r = home(s)
        for k in range(1, HEADS):
            peer = (head + k) % HEADS
            arrived(rbuf.at[s, peer], cr.at[s, peer])
        total = cbuf[s, r, y].astype(jnp.float32)
        for k in range(1, HEADS):
            total = total + rbuf[s, (head + k) % HEADS].astype(jnp.float32)
        fsrc[s] = total.astype(jnp.bfloat16)
        here = is_here(s)

        @pl.when(here)
        def _():
            spot[...] = fsrc[s]

        @pl.when(jnp.logical_not(here))
        def _():
            f_copy(s).start()

    @pl.loop(0, NZ)
    def _(s):
        @pl.when(s - 1 >= done)
        def _():
            forward(s - 1)

        multiply(s)

        @pl.when(s >= 2)
        def _():
            gather(s - 2)

    gather(6)
    gather(7)

    for p in range(4):
        for b in range(2):
            @pl.when((p != j) | (j != y) | (b != xh))
            def _():
                arrived(fin.at[pl.ds((2 * p + b) * HALF, HALF), :], fr.at[2 * p + b])
    out_ref[...] = fin[...].T

    for k in range(1, NZ):
        @pl.when(z + k < NZ)
        def _():
            z_copy(k).wait_send()

    @pl.loop(0, z + 1)
    def _(zs):
        @pl.when(zs < z)
        def _():
            for k in range(1, 4):
                y_copy(zs, k).wait_send()
        for each in x_copies(zs):
            each.wait_send()
        core_copy(zs, j, 0).wait_send()
        core_copy(zs, opp, 1).wait_send()

    @pl.loop(0, 7)
    def _(u):
        ring_up(u).wait_send()
        ring_down(u).wait_send()

    for c in range(2):
        a_x(c).wait_send()
        a_core(c).wait_send()
        a_forward(c).wait_send()

    @pl.loop(0, NZ)
    def _(s):
        each_copy(s, lambda each: each.wait_send())

        @pl.when(jnp.logical_not(is_here(s)))
        def _():
            f_copy(s).wait_send()


def on_device(queries, compressed, latent_gain, w_uk, w_uv, w_out):
    dma = pltpu.SemaphoreType.DMA
    bf = jnp.bfloat16
    return pl.pallas_call(
        kernel,
        out_shape=jax.ShapeDtypeStruct((ROWS, NZ * HALF), bf),
        in_specs=[pl.BlockSpec(memory_space=pltpu.VMEM)] * 6,
        out_specs=pl.BlockSpec(memory_space=pltpu.VMEM),
        scratch_shapes=[
            pltpu.VMEM((NZ, STRIP, WIDE), bf),
            pltpu.VMEM((NZ, 2, HALF, HEADS * NOPE), bf),
            pltpu.VMEM((WIDE, TOTAL), bf),
            pltpu.VMEM((HEADS * NOPE, LATENT), bf),
            pltpu.VMEM((1, TOTAL), jnp.float32),
            pltpu.VMEM((1, TOTAL), jnp.float32),
            pltpu.VMEM((LATENT, TOTAL), jnp.float32),
            pltpu.VMEM((HEADS * NOPE, STRIP), bf),
            pltpu.VMEM((NZ, 2, 4, HALF, ROWS), bf),
            pltpu.VMEM((NZ, HEADS, HALF, ROWS), bf),
            pltpu.VMEM((NZ, HALF, ROWS), bf),
            pltpu.VMEM((NZ * HALF, ROWS), bf),
            dma((NZ,)), dma((NZ,)),
            dma((NZ, 3)), dma((NZ, 3)),
            dma((NZ, 2)), dma((NZ, 2)),
            dma((NZ, 2)), dma((NZ, 2)),
            dma((7,)), dma((7,)),
            dma((7,)), dma((7,)),
            dma((2,)), dma((2,)),
            dma((2,)), dma((2,)),
            dma((2,)), dma((2,)),
            dma((NZ, 2, 4)), dma((NZ, HEADS)),
            dma((NZ,)), dma((NZ,)),
        ],
        compiler_params=pltpu.CompilerParams(
            collective_id=0, has_side_effects=True, vmem_limit_bytes=56 * 1024 * 1024),
        name="layer",
    )(queries, compressed, latent_gain.reshape(1, LATENT), w_uk, w_uv, w_out)


def solution(mesh):
    return jax.shard_map(
        on_device,
        mesh=mesh,
        in_specs=(
            P("ctx", "head"),
            P("ctx", None),
            P(),
            P(None, "head"),
            P(None, "head"),
            P("head", "ctx"),
        ),
        out_specs=P("ctx", "head"),
        check_vma=False,
    )
```

time: 260 us -> 99.4 us (0.38)
  the two profiles are of different devices: /device:TPU:1 before, /device:TPU:17 now
where the time goes in v2:
time: 99.4 us; the launch traced here: 99.2 us
  Pallas kernels  93.8 us (94%)
  local copies, waits for them, and re-layouts  5.37 us (5%)
    pallas_call x1, Pallas kernels, on_device(): pl.pallas_call(kernel, out_shape=jax.ShapeDtypeStruct((ROWS, NZ * HALF),...  93.8 us
    unnamed x3, local copies, waits for them, and re-layouts  5.37 us

profile of v2, /device:TPU:17, one launch (start us, length us, event | category | flops | bytes accessed | tf_op | source)
XLA Modules:
  0.0 99.2 jit_solution(17236927894208545783)
XLA Ops:
  0.0 1.7 %copy.7.comp_ref = bf16[128,576]{1,0:T(8,128)(2,1)} copy(bf16[128,576]{0,1:T(8,128)(2,1)} %param.7) | data formatting | bytes 294912 | tf_op args[1]
  1.7 2.0 %copy.8.w_ref = bf16[1024,224]{1,0:T(8,128)(2,1)} copy(bf16[1024,224]{0,1:T(8,128)(2,1)} %param.11) | data formatting | bytes 917504 | tf_op args[5]
  3.7 93.8 %layer.1 = bf16[128,896]{1,0:T(8,128)(2,1)} custom-call(bf16[128,1536]{1,0:T(8,128)(2,1)} %q_ref.1, bf16[128,576]{1,0:T(8,128)(2,1)} %copy.7.comp_ref, f32[1,512]{1,0:T(1,128)} %bitcast.1, bf16[512,1024]{1,0:T(8,128)(2,1)} %uk_ref.1, bf16[512,1024]{1,0:T(8,128)(2,1)} %uv_ref.1, bf16[1024,224]{1,0:T(8,128)(2,1)} %copy.8.w_ref), custom_call_target="tpu_custom_call" | custom-call | tf_op jit(solution)/shard_map/layer/pallas_call | solution.py:396
  97.6 1.6 %copy.10 = bf16[128,896]{1,0:T(8,128)(2,1)} copy(bf16[128,896]{1,0:T(8,128)(2,1)} %layer.1) | data formatting | bytes 458752

commit v3 on v2

--- a/solution.py
+++ b/solution.py
@@ -30,8 +30,8 @@
 
 def kernel(q_ref, comp_ref, gain_ref, uk_ref, uv_ref, w_ref, out_ref,
            lat, ball, qt, uvt, m_ref, l_ref, acc, abuf, cbuf, rbuf, fsrc, fin,
-           s1s, s1r, s2s, s2r, s3s, s3r, s4s, s4r, brs, brr, bls, blr,
-           axs, axr, acs, acr, afs, afr, cs, cr, fs, fr):
+           s1s, s1r, s2s, s2r, s3s, s3r, s4s, s4r, sws, swr, brs, brr, bls, blr,
+           axs, axr, ars, arr, acs, acr, cs, cr, fs, fr):
     ctx = lax.axis_index("ctx")
     head = lax.axis_index("head")
     z = ctx // 4
@@ -43,10 +43,12 @@
     sib = j + 1 - 2 * (j % 2)
     opp = (j + 2) % 4
     opp_sib = (sib + 2) % 4
-    x_lo = (base + opp, head)
+    up_xh = (xh + xl) % 2
+    down_xh = 1 - up_xh
+    over = (ctx, 2 * y + 1 - xh)
     core = (base + sib, head)
-    x_up = (base + opp, 2 * y + (xh + xl) % 2)
-    x_down = (base + opp, 2 * y + (xh + xl + 1) % 2)
+    x_up = (base + opp, 2 * y + up_xh)
+    x_down = (base + opp, 2 * y + down_xh)
     z_up = (4 * ((z + 1) % NZ) + j, head)
     z_down = (4 * ((z + 7) % NZ) + j, head)
 
@@ -67,8 +69,9 @@
 
     for k in range(1, NZ):
         greet((4 * ((z + k) % NZ) + j, head))
-    for k in range(1, HEADS):
-        greet((ctx, (head + k) % HEADS))
+    for k in range(1, 4):
+        greet((ctx, 2 * ((y + k) % 4) + xh))
+    greet(over)
     greet(x_up)
     greet(x_down)
     greet(core)
@@ -78,18 +81,17 @@
             def _():
                 greet((base + p, 2 * j + b))
 
-    own = comp_ref[:, :LATENT].astype(jnp.float32)
+    comp = comp_ref[...].T
+    own = comp[:, :LATENT].astype(jnp.float32)
     mean_square = jnp.mean(own * own, axis=1, keepdims=True)
     normed = (own * lax.rsqrt(mean_square + 1e-06) * gain_ref[...]).astype(jnp.bfloat16)
     mine = pl.ds(al(j * ROWS, ROWS), ROWS)
     lat[z, mine, :LATENT] = normed
     lat[z, mine, LATENT:] = jnp.concatenate(
-        [comp_ref[:, LATENT:], jnp.zeros((ROWS, WIDE - LATENT - ROPE), jnp.bfloat16)], axis=1)
-    wt = w_ref[...].T
-    ball[z, 0] = wt[:HALF]
-    ball[z, 1] = wt[HALF:]
-
-    pl.semaphore_wait(barrier, jnp.where(j == y, 24, 25))
+        [comp[:, LATENT:], jnp.zeros((ROWS, WIDE - LATENT - ROPE), jnp.bfloat16)], axis=1)
+    ball[z, xh] = w_ref[pl.ds(al(xh * HALF, 16), HALF), :]
+
+    pl.semaphore_wait(barrier, jnp.where(j == y, 21, 22))
 
     def rows_of(zs, member, start, count):
         return lat.at[zs, pl.ds(al(member * ROWS + start, 16), count), :]
@@ -143,17 +145,19 @@
         arrived(rows_of(zs, sib, 0, ROWS), s4r.at[zs, 0])
         arrived(rows_of(zs, opp_sib, 0, ROWS), s4r.at[zs, 1])
 
+    swap = copy(w_ref.at[pl.ds(al((1 - xh) * HALF, 16), HALF), :], ball.at[z, xh], sws, swr, over)
+
     def ring_up(u):
-        part = ball.at[(z + NZ - u // 2) % NZ, u % 2]
+        part = ball.at[(z + NZ - u // 2) % NZ, (xh + u) % 2]
         return copy(part, part, brs.at[u], brr.at[u], z_up)
 
     def ring_down(u):
-        part = ball.at[(z + u // 2) % NZ, 1 - u % 2]
+        part = ball.at[(z + u // 2) % NZ, (xh + u + u // 6) % 2]
         return copy(part, part, bls.at[u], blr.at[u], z_down)
 
     def ring_arrived(k):
-        arrived(ball.at[(z + 7 - k // 2) % NZ, k % 2], brr.at[k])
-        arrived(ball.at[(z + 1 + k // 2) % NZ, 1 - k % 2], blr.at[k])
+        arrived(ball.at[(z + 7 - k // 2) % NZ, (xh + k) % 2], brr.at[k])
+        arrived(ball.at[(z + 1 + k // 2) % NZ, (xh + k + k // 6) % 2], blr.at[k])
 
     def forward(k):
         ring_arrived(k)
@@ -161,7 +165,14 @@
         @pl.when(k < 5)
         def _():
             ring_up(k + 2).start()
+
+        @pl.when(k < 4)
+        def _():
             ring_down(k + 2).start()
+
+        @pl.when(k == 5)
+        def _():
+            ring_down(6).start()
 
     def when_in(d, act):
         @pl.when(d <= z)
@@ -169,9 +180,7 @@
             act(d)
 
     stage2(0, wait=False)
-    for u in range(2):
-        ring_up(u).start()
-        ring_down(u).start()
+    swap.start()
 
     def absorb(h):
         lanes = slice(h * ROWS, (h + 1) * ROWS)
@@ -184,9 +193,21 @@
     qt[LATENT + ROPE:, :] = jnp.zeros((WIDE - LATENT - ROPE, TOTAL), jnp.bfloat16)
     for h in range(HEADS):
         absorb(h)
+    ring_up(0).start()
+    ring_down(0).start()
     when_in(1, stage1)
     when_in(2, stage1)
     uvt[...] = uv_ref[...].T
+    when_in(3, stage1)
+    stage3(0)
+    arrived(ball.at[z, 1 - xh], swr)
+    ring_up(1).start()
+    ring_down(1).start()
+    when_in(1, stage2)
+    when_in(4, stage1)
+    when_in(2, stage2)
+    when_in(5, stage1)
+    when_in(3, stage2)
 
     def visit(zs, first):
         block = lat[zs]
@@ -222,106 +243,123 @@
         rest(s, 0)
         rest(later, 1)
 
-    when_in(1, stage2)
-    stage3(0)
-    when_in(3, stage1)
-    when_in(2, stage2)
+    def ahead(i):
+        when_in(i + 6, stage1)
+        when_in(i + 4, stage2)
+
     when_in(1, stage3)
     stage4(0)
     visit(z, True)
+    ahead(0)
+    forward(0)
 
     @pl.loop(1, z + 1)
     def _(i):
-        when_in(i + 3, stage1)
-        when_in(i + 2, stage2)
         when_in(i + 1, stage3)
         stage4(i)
         visit(z - i, False)
-
-        @pl.when(i % 2 == 0)
-        def _():
-            forward(i // 2 - 1)
-
-    done = z // 2
-
-    def piece(member, c):
-        return abuf.at[pl.ds(c * CHUNK, CHUNK), pl.ds(al(member * ROWS, ROWS), ROWS)]
-
-    def a_x(c):
-        return copy(piece(j, c), piece(j, c), axs.at[c], axr.at[c], x_lo)
-
-    def a_core(c):
-        return copy(piece(j, c), piece(j, c), acs.at[c], acr.at[c], core)
-
-    def a_forward(c):
-        return copy(piece(opp, c), piece(opp, c), afs.at[c], afr.at[c], core)
+        ahead(i)
+
+        @pl.when(i % 2 == 1)
+        def _():
+            forward((i + 1) // 2)
+
+    done = jnp.maximum(2, 1 + (z + 1) // 2)
+
+    def piece(across, member, c, start=0, count=CHUNK):
+        return abuf.at[across, pl.ds(c * CHUNK + start, count), pl.ds(al(member * ROWS, ROWS), ROWS)]
+
+    def a_sends(c):
+        part = piece(xh, j, c)
+        return (copy(part, part, axs.at[c, 0], axr.at[c, 0], x_up),
+                copy(part, part, axs.at[c, 1], axr.at[c, 1], x_down),
+                copy(part, part, acs.at[c, 0], acr.at[c, 0], core))
+
+    def a_from_down(c):
+        part, half = piece(down_xh, opp, c), piece(down_xh, opp, c, 0, CHUNK // 2)
+        return (copy(half, half, ars.at[c, 0], arr.at[c, 0], x_up),
+                copy(part, part, acs.at[c, 1], acr.at[c, 1], core))
+
+    def a_from_up(c):
+        part, half = piece(up_xh, opp, c), piece(up_xh, opp, c, CHUNK // 2, CHUNK // 2)
+        return (copy(half, half, ars.at[c, 1], arr.at[c, 1], x_down),
+                copy(part, part, acs.at[c, 2], acr.at[c, 2], core))
+
+    def a_across(c):
+        part = piece(1 - xh, j, c)
+        return copy(part, part, acs.at[c, 3], acr.at[c, 3], core)
 
     for c in range(2):
         for h in range(c * 4, c * 4 + 4):
             lanes = slice(h * ROWS, (h + 1) * ROWS)
             o = (acc[:, lanes] / l_ref[:, lanes]).astype(jnp.bfloat16)
             a = jnp.dot(uvt[h * NOPE:(h + 1) * NOPE, :], o, preferred_element_type=jnp.float32)
-            abuf[h * NOPE:(h + 1) * NOPE, mine] = a.astype(jnp.bfloat16)
-        a_x(c).start()
-        a_core(c).start()
+            abuf[xh, h * NOPE:(h + 1) * NOPE, mine] = a.astype(jnp.bfloat16)
+        for each in a_sends(c):
+            each.start()
     for c in range(2):
-        arrived(piece(opp, c), axr.at[c])
-        a_forward(c).start()
+        arrived(piece(down_xh, opp, c), axr.at[c, 0])
+        for each in a_from_down(c):
+            each.start()
+        arrived(piece(up_xh, opp, c), axr.at[c, 1])
+        for each in a_from_up(c):
+            each.start()
+
+    @pl.when(z == 0)
+    def _():
+        forward(1)
+
     for c in range(2):
-        arrived(piece(sib, c), acr.at[c])
+        arrived(piece(1 - xh, j, c, 0, CHUNK // 2), arr.at[c, 0])
+        arrived(piece(1 - xh, j, c, CHUNK // 2, CHUNK // 2), arr.at[c, 1])
+        a_across(c).start()
     for c in range(2):
-        arrived(piece(opp_sib, c), afr.at[c])
-
-    def places(s):
-        u = jnp.maximum(s - 1, 0)
+        arrived(piece(xh, sib, c), acr.at[c, 0])
+        arrived(piece(down_xh, opp_sib, c), acr.at[c, 1])
+        arrived(piece(up_xh, opp_sib, c), acr.at[c, 2])
+        arrived(piece(1 - xh, sib, c), acr.at[c, 3])
+
+    def home(s):
         far = (s + 1) // 2
-        up = (z + NZ - far) % NZ
-        down = (z + far) % NZ
-        return up, down, u % 2
-
-    def c_copy(s, r, t, b):
-        return copy(cbuf.at[s, r, t], rbuf.at[s, head], cs.at[s, r, t], cr.at[s, head], (ctx, 2 * t + b))
+        return (z + NZ + far * (1 - 2 * (s % 2))) % NZ
+
+    def c_copy(s, t):
+        return copy(cbuf.at[s, t], rbuf.at[s, y], cs.at[s, t], cr.at[s, y], (ctx, 2 * t + xh))
 
     def each_copy(s, act):
-        odd = places(s)[2]
-        for r in range(2):
-            b = (odd + r) % 2
+        for t in range(4):
+            @pl.when(t != y)
+            def _():
+                act(c_copy(s, t))
+
+    def multiply(slots):
+        ct = None
+        for across in range(2):
+            blocks = [ball[home(s), across] for s in slots]
+            rows = jnp.concatenate(blocks, axis=0) if len(blocks) > 1 else blocks[0]
+            part = jnp.dot(rows, abuf[across], preferred_element_type=jnp.float32)
+            ct = part if ct is None else ct + part
+        ct = ct.astype(jnp.bfloat16)
+        for r, s in enumerate(slots):
             for t in range(4):
-                @pl.when((t != y) | (b != xh))
-                def _():
-                    act(c_copy(s, r, t, b))
-
-    def multiply(s):
-        up, down, odd = places(s)
-        both = jnp.concatenate([ball[up, odd], ball[down, 1 - odd]], axis=0)
-        ct = jnp.dot(both, abuf[...], preferred_element_type=jnp.float32).astype(jnp.bfloat16)
-        for r in range(2):
-            for t in range(4):
-                cbuf[s, r, t] = ct[r * HALF:(r + 1) * HALF, t * ROWS:(t + 1) * ROWS]
-        each_copy(s, lambda each: each.start())
-
-    def home(s):
-        up, down, odd = places(s)
-        same = (odd + xh) % 2
-        return up * (1 - same) + down * same, same
+                cbuf[s, t] = ct[r * HALF:(r + 1) * HALF, t * ROWS:(t + 1) * ROWS]
+            each_copy(s, lambda each: each.start())
 
     spot = fin.at[pl.ds(al((2 * j + xh) * HALF, HALF), HALF), :]
 
     def f_copy(s):
-        n, _ = home(s)
-        return copy(fsrc.at[s], spot, fs.at[s], fr.at[2 * j + xh], (base + y, n))
+        return copy(fsrc.at[s], spot, fs.at[s], fr.at[2 * j + xh], (base + y, home(s)))
 
     def is_here(s):
-        return (y == j) & (home(s)[0] == head)
+        return (y == j) & (home(s) == head)
 
     def gather(s):
-        n, r = home(s)
-        for k in range(1, HEADS):
-            peer = (head + k) % HEADS
+        for k in range(1, 4):
+            peer = (y + k) % 4
             arrived(rbuf.at[s, peer], cr.at[s, peer])
-        total = cbuf[s, r, y].astype(jnp.float32)
-        for k in range(1, HEADS):
-            total = total + rbuf[s, (head + k) % HEADS].astype(jnp.float32)
+        total = cbuf[s, y].astype(jnp.float32)
+        for k in range(1, 4):
+            total = total + rbuf[s, (y + k) % 4].astype(jnp.float32)
         fsrc[s] = total.astype(jnp.bfloat16)
         here = is_here(s)
 
@@ -333,27 +371,39 @@
         def _():
             f_copy(s).start()
 
-    @pl.loop(0, NZ)
-    def _(s):
-        @pl.when(s - 1 >= done)
-        def _():
-            forward(s - 1)
-
-        multiply(s)
-
-        @pl.when(s >= 2)
-        def _():
-            gather(s - 2)
-
-    gather(6)
-    gather(7)
+    def reach(k):
+        @pl.when(k >= done)
+        def _():
+            forward(k)
+
+    multiply([0])
+
+    @pl.loop(1, 4)
+    def _(g):
+        reach(2 * g - 2)
+        reach(2 * g - 1)
+        multiply([2 * g - 1, 2 * g])
+
+        @pl.when(g == 1)
+        def _():
+            gather(0)
+
+        @pl.when(g > 1)
+        def _():
+            gather(2 * g - 3)
+            gather(2 * g - 2)
+
+    reach(6)
+    multiply([7])
+    for s in range(5, 8):
+        gather(s)
 
     for p in range(4):
         for b in range(2):
             @pl.when((p != j) | (j != y) | (b != xh))
             def _():
                 arrived(fin.at[pl.ds((2 * p + b) * HALF, HALF), :], fr.at[2 * p + b])
-    out_ref[...] = fin[...].T
+    out_ref[...] = fin[...]
 
     for k in range(1, NZ):
         @pl.when(z + k < NZ)
@@ -371,15 +421,16 @@
         core_copy(zs, j, 0).wait_send()
         core_copy(zs, opp, 1).wait_send()
 
+    swap.wait_send()
+
     @pl.loop(0, 7)
     def _(u):
         ring_up(u).wait_send()
         ring_down(u).wait_send()
 
     for c in range(2):
-        a_x(c).wait_send()
-        a_core(c).wait_send()
-        a_forward(c).wait_send()
+        for each in a_sends(c) + a_from_down(c) + a_from_up(c) + (a_across(c),):
+            each.wait_send()
 
     @pl.loop(0, NZ)
     def _(s):
@@ -395,7 +446,7 @@
     bf = jnp.bfloat16
     return pl.pallas_call(
         kernel,
-        out_shape=jax.ShapeDtypeStruct((ROWS, NZ * HALF), bf),
+        out_shape=jax.ShapeDtypeStruct((NZ * HALF, ROWS), bf),
         in_specs=[pl.BlockSpec(memory_space=pltpu.VMEM)] * 6,
         out_specs=pl.BlockSpec(memory_space=pltpu.VMEM),
         scratch_shapes=[
@@ -406,27 +457,28 @@
             pltpu.VMEM((1, TOTAL), jnp.float32),
             pltpu.VMEM((1, TOTAL), jnp.float32),
             pltpu.VMEM((LATENT, TOTAL), jnp.float32),
-            pltpu.VMEM((HEADS * NOPE, STRIP), bf),
-            pltpu.VMEM((NZ, 2, 4, HALF, ROWS), bf),
-            pltpu.VMEM((NZ, HEADS, HALF, ROWS), bf),
+            pltpu.VMEM((2, HEADS * NOPE, STRIP), bf),
+            pltpu.VMEM((NZ, 4, HALF, ROWS), bf),
+            pltpu.VMEM((NZ, 4, HALF, ROWS), bf),
             pltpu.VMEM((NZ, HALF, ROWS), bf),
             pltpu.VMEM((NZ * HALF, ROWS), bf),
             dma((NZ,)), dma((NZ,)),
             dma((NZ, 3)), dma((NZ, 3)),
             dma((NZ, 2)), dma((NZ, 2)),
             dma((NZ, 2)), dma((NZ, 2)),
+            dma, dma,
             dma((7,)), dma((7,)),
             dma((7,)), dma((7,)),
-            dma((2,)), dma((2,)),
-            dma((2,)), dma((2,)),
-            dma((2,)), dma((2,)),
-            dma((NZ, 2, 4)), dma((NZ, HEADS)),
+            dma((2, 2)), dma((2, 2)),
+            dma((2, 2)), dma((2, 2)),
+            dma((2, 4)), dma((2, 4)),
+            dma((NZ, 4)), dma((NZ, 4)),
             dma((NZ,)), dma((NZ,)),
         ],
         compiler_params=pltpu.CompilerParams(
             collective_id=0, has_side_effects=True, vmem_limit_bytes=56 * 1024 * 1024),
         name="layer",
-    )(queries, compressed, latent_gain.reshape(1, LATENT), w_uk, w_uv, w_out)
+    )(queries, compressed.T, latent_gain.reshape(1, LATENT), w_uk, w_uv, w_out.T).T
 
 
 def solution(mesh):

time: 99.4 us -> 86.9 us (0.87)
  the two profiles are of different devices: /device:TPU:17 before, /device:TPU:200 now
where the time goes in v3:
time: 86.9 us; the launch traced here: 86.8 us
  Pallas kernels  85 us (98%)
  local copies, waits for them, and re-layouts  1.76 us (2%)
    pallas_call x1, Pallas kernels, on_device(): pl.pallas_call(kernel, out_shape=jax.ShapeDtypeStruct((NZ * HALF, ROWS),...  85 us
    transpose x1, local copies, waits for them, and re-layouts, on_device(): return pl.pallas_call(kernel, out_shape=jax.ShapeDtypeStruct((NZ * HALF,...  1.76 us

profile of v3, /device:TPU:200, one launch (start us, length us, event | category | flops | bytes accessed | tf_op | source)
XLA Modules:
  0.0 86.8 jit_solution(8301639745651351720)
XLA Ops:
  0.0 85.0 %layer.1 = bf16[896,128]{1,0:T(8,128)(2,1)} custom-call(bf16[128,1536]{1,0:T(8,128)(2,1)} %q_ref.1, bf16[576,128]{1,0:T(8,128)(2,1)} %bitcast.6, f32[1,512]{1,0:T(1,128)} %bitcast.7, bf16[512,1024]{1,0:T(8,128)(2,1)} %uk_ref.1, bf16[512,1024]{1,0:T(8,128)(2,1)} %uv_ref.1, bf16[224,1024]{1,0:T(8,128)(2,1)} %bitcast.5), custom_call_target="tpu_custom_call" | custom-call | tf_op jit(solution)/shard_map/layer/pallas_call | solution.py:447
  85.0 1.8 %copy.7 = bf16[128,896]{1,0:T(8,128)(2,1)} copy(bf16[128,896]{0,1:T(8,128)(2,1)} %bitcast.4) | data formatting | bytes 458752 | tf_op jit(solution)/shard_map/transpose | solution.py:481

commit v4 on v3

--- a/solution.py
+++ b/solution.py
@@ -28,7 +28,8 @@
     return pl.multiple_of(value, unit)
 
 
-def kernel(q_ref, comp_ref, gain_ref, uk_ref, uv_ref, w_ref, out_ref,
+def kernel(q_hbm, comp_hbm, gain_ref, uk_hbm, uv_hbm, w_hbm, out_ref,
+           q_ref, comp_ref, uk_ref, uv_ref, w_ref, loads,
            lat, ball, qt, uvt, m_ref, l_ref, acc, abuf, cbuf, rbuf, fsrc, fin,
            s1s, s1r, s2s, s2r, s3s, s3r, s4s, s4r, sws, swr, brs, brr, bls, blr,
            axs, axr, ars, arr, acs, acr, cs, cr, fs, fr):
@@ -62,6 +63,11 @@
     def left(src, send):
         copy(src, src, send, send, core).wait_send()
 
+    fetch = [pltpu.make_async_copy(a, b, loads.at[n]) for n, (a, b) in enumerate((
+        (comp_hbm, comp_ref), (w_hbm, w_ref), (q_hbm, q_ref), (uk_hbm, uk_ref), (uv_hbm, uv_ref)))]
+    for each in fetch:
+        each.start()
+
     barrier = pltpu.get_barrier_semaphore()
 
     def greet(device):
@@ -81,6 +87,7 @@
             def _():
                 greet((base + p, 2 * j + b))
 
+    fetch[0].wait()
     comp = comp_ref[...].T
     own = comp[:, :LATENT].astype(jnp.float32)
     mean_square = jnp.mean(own * own, axis=1, keepdims=True)
@@ -89,6 +96,7 @@
     lat[z, mine, :LATENT] = normed
     lat[z, mine, LATENT:] = jnp.concatenate(
         [comp[:, LATENT:], jnp.zeros((ROWS, WIDE - LATENT - ROPE), jnp.bfloat16)], axis=1)
+    fetch[1].wait()
     ball[z, xh] = w_ref[pl.ds(al(xh * HALF, 16), HALF), :]
 
     pl.semaphore_wait(barrier, jnp.where(j == y, 21, 22))
@@ -179,8 +187,10 @@
         def _():
             act(d)
 
+    swap.start()
     stage2(0, wait=False)
-    swap.start()
+    ring_up(0).start()
+    ring_down(0).start()
 
     def absorb(h):
         lanes = slice(h * ROWS, (h + 1) * ROWS)
@@ -191,25 +201,26 @@
         qt[LATENT:LATENT + ROPE, lanes] = qr.T.astype(jnp.bfloat16)
 
     qt[LATENT + ROPE:, :] = jnp.zeros((WIDE - LATENT - ROPE, TOTAL), jnp.bfloat16)
+    fetch[2].wait()
+    fetch[3].wait()
     for h in range(HEADS):
         absorb(h)
-    ring_up(0).start()
-    ring_down(0).start()
-    when_in(1, stage1)
-    when_in(2, stage1)
+    fetch[4].wait()
     uvt[...] = uv_ref[...].T
-    when_in(3, stage1)
-    stage3(0)
+    for d in range(1, 4):
+        when_in(d, stage1)
     arrived(ball.at[z, 1 - xh], swr)
     ring_up(1).start()
     ring_down(1).start()
     when_in(1, stage2)
     when_in(4, stage1)
+    when_in(5, stage1)
+    forward(0)
     when_in(2, stage2)
-    when_in(5, stage1)
+    stage3(0)
     when_in(3, stage2)
 
-    def visit(zs, first):
+    def visit(zs, first, chunk=None):
         block = lat[zs]
         turned = block[:, :LATENT].T
 
@@ -238,33 +249,43 @@
                 l_ref[:, lanes] = l_ref[:, lanes] * alpha + total
                 acc[:, lanes] = acc[:, lanes] * alpha + part
 
-        s = score(0)
-        later = score(1)
-        rest(s, 0)
-        rest(later, 1)
+        if chunk is None:
+            s = score(0)
+            later = score(1)
+            rest(s, 0)
+            rest(later, 1)
+        else:
+            rest(score(chunk), chunk)
 
     def ahead(i):
         when_in(i + 6, stage1)
         when_in(i + 4, stage2)
 
-    when_in(1, stage3)
     stage4(0)
     visit(z, True)
+    when_in(1, stage3)
     ahead(0)
-    forward(0)
-
-    @pl.loop(1, z + 1)
+    forward(1)
+
+    @pl.loop(1, z)
     def _(i):
         when_in(i + 1, stage3)
         stage4(i)
         visit(z - i, False)
         ahead(i)
 
-        @pl.when(i % 2 == 1)
-        def _():
-            forward((i + 1) // 2)
-
-    done = jnp.maximum(2, 1 + (z + 1) // 2)
+        @pl.when((i == 2) | (i == 4))
+        def _():
+            forward(1 + i // 2)
+
+    def last_visit(c):
+        @pl.when(z >= 1)
+        def _():
+            if c == 0:
+                stage4(z)
+            visit(0, False, c)
+
+    done = jnp.minimum(1 + (z + 1) // 2, 4)
 
     def piece(across, member, c, start=0, count=CHUNK):
         return abuf.at[across, pl.ds(c * CHUNK + start, count), pl.ds(al(member * ROWS, ROWS), ROWS)]
@@ -290,6 +311,7 @@
         return copy(part, part, acs.at[c, 3], acr.at[c, 3], core)
 
     for c in range(2):
+        last_visit(c)
         for h in range(c * 4, c * 4 + 4):
             lanes = slice(h * ROWS, (h + 1) * ROWS)
             o = (acc[:, lanes] / l_ref[:, lanes]).astype(jnp.bfloat16)
@@ -297,6 +319,10 @@
             abuf[xh, h * NOPE:(h + 1) * NOPE, mine] = a.astype(jnp.bfloat16)
         for each in a_sends(c):
             each.start()
+        if c == 0:
+            @pl.when(z >= 1)
+            def _():
+                forward(done)
     for c in range(2):
         arrived(piece(down_xh, opp, c), axr.at[c, 0])
         for each in a_from_down(c):
@@ -305,14 +331,15 @@
         for each in a_from_up(c):
             each.start()
 
-    @pl.when(z == 0)
+    @pl.when(z <= 4)
     def _():
-        forward(1)
+        forward(done + 1)
 
     for c in range(2):
         arrived(piece(1 - xh, j, c, 0, CHUNK // 2), arr.at[c, 0])
         arrived(piece(1 - xh, j, c, CHUNK // 2, CHUNK // 2), arr.at[c, 1])
         a_across(c).start()
+    forward(jnp.minimum(done + 2, 5))
     for c in range(2):
         arrived(piece(xh, sib, c), acr.at[c, 0])
         arrived(piece(down_xh, opp_sib, c), acr.at[c, 1])
@@ -372,7 +399,7 @@
             f_copy(s).start()
 
     def reach(k):
-        @pl.when(k >= done)
+        @pl.when(k >= jnp.minimum(done + 3, 6))
         def _():
             forward(k)
 
@@ -447,9 +474,15 @@
     return pl.pallas_call(
         kernel,
         out_shape=jax.ShapeDtypeStruct((NZ * HALF, ROWS), bf),
-        in_specs=[pl.BlockSpec(memory_space=pltpu.VMEM)] * 6,
+        in_specs=[pl.BlockSpec(memory_space=pltpu.VMEM if n == 2 else pl.ANY) for n in range(6)],
         out_specs=pl.BlockSpec(memory_space=pltpu.VMEM),
         scratch_shapes=[
+            pltpu.VMEM((ROWS, HEADS * HD), bf),
+            pltpu.VMEM((LATENT + ROPE, ROWS), bf),
+            pltpu.VMEM((LATENT, HEADS * NOPE), bf),
+            pltpu.VMEM((LATENT, HEADS * NOPE), bf),
+            pltpu.VMEM((2 * HALF, HEADS * NOPE), bf),
+            dma((5,)),
             pltpu.VMEM((NZ, STRIP, WIDE), bf),
             pltpu.VMEM((NZ, 2, HALF, HEADS * NOPE), bf),
             pltpu.VMEM((WIDE, TOTAL), bf),

time: 86.9 us -> 80.6 us (0.928)
  the two profiles are of different devices: /device:TPU:200 before, /device:TPU:239 now
where the time goes in v4:
time: 80.6 us; the launch traced here: 80.5 us
  Pallas kernels  78.7 us (98%)
  local copies, waits for them, and re-layouts  1.76 us (2%)
    pallas_call x1, Pallas kernels, on_device(): pl.pallas_call(kernel, out_shape=jax.ShapeDtypeStruct((NZ * HALF, ROWS),...  78.7 us
    transpose x1, local copies, waits for them, and re-layouts, on_device(): return pl.pallas_call(kernel, out_shape=jax.ShapeDtypeStruct((NZ * HALF,...  1.76 us

profile of v4, /device:TPU:239, one launch (start us, length us, event | category | flops | bytes accessed | tf_op | source)
XLA Modules:
  0.0 80.5 jit_solution(10249043316467522048)
XLA Ops:
  0.0 78.7 %layer.1 = bf16[896,128]{1,0:T(8,128)(2,1)} custom-call(bf16[128,1536]{1,0:T(8,128)(2,1)} %q_hbm.1, bf16[576,128]{1,0:T(8,128)(2,1)} %bitcast.6, f32[1,512]{1,0:T(1,128)} %bitcast.7, bf16[512,1024]{1,0:T(8,128)(2,1)} %uk_hbm.1, bf16[512,1024]{1,0:T(8,128)(2,1)} %uv_hbm.1, bf16[224,1024]{1,0:T(8,128)(2,1)} %bitcast.5), custom_call_target="tpu_custom_call" | custom-call | tf_op jit(solution)/shard_map/layer/pallas_call | solution.py:474
  78.7 1.8 %copy.7 = bf16[128,896]{1,0:T(8,128)(2,1)} copy(bf16[128,896]{0,1:T(8,128)(2,1)} %bitcast.4) | data formatting | bytes 458752 | tf_op jit(solution)/shard_map/transpose | solution.py:514

commit v5 on v4

--- a/solution.py
+++ b/solution.py
@@ -17,6 +17,7 @@
 STRIP = 4 * ROWS
 TOTAL = HEADS * ROWS
 CHUNK = 512
+PART = 256
 HALF = 112
 NZ = 8
 SCALE = HD ** -0.5 * math.log2(math.e)
@@ -189,8 +190,6 @@
 
     swap.start()
     stage2(0, wait=False)
-    ring_up(0).start()
-    ring_down(0).start()
 
     def absorb(h):
         lanes = slice(h * ROWS, (h + 1) * ROWS)
@@ -209,16 +208,22 @@
     uvt[...] = uv_ref[...].T
     for d in range(1, 4):
         when_in(d, stage1)
+    for k in range(1, NZ):
+        @pl.when(z + k < NZ)
+        def _():
+            z_copy(k).wait_send()
+    ring_up(0).start()
+    ring_down(0).start()
     arrived(ball.at[z, 1 - xh], swr)
     ring_up(1).start()
     ring_down(1).start()
     when_in(1, stage2)
     when_in(4, stage1)
     when_in(5, stage1)
-    forward(0)
     when_in(2, stage2)
     stage3(0)
     when_in(3, stage2)
+    forward(0)
 
     def visit(zs, first, chunk=None):
         block = lat[zs]
@@ -265,7 +270,6 @@
     visit(z, True)
     when_in(1, stage3)
     ahead(0)
-    forward(1)
 
     @pl.loop(1, z)
     def _(i):
@@ -274,9 +278,9 @@
         visit(z - i, False)
         ahead(i)
 
-        @pl.when((i == 2) | (i == 4))
-        def _():
-            forward(1 + i // 2)
+        @pl.when(jnp.where(z >= 5, (i == 2) | (i == 4), i % 2 == 1))
+        def _():
+            forward((i + 1) // 2)
 
     def last_visit(c):
         @pl.when(z >= 1)
@@ -285,10 +289,10 @@
                 stage4(z)
             visit(0, False, c)
 
-    done = jnp.minimum(1 + (z + 1) // 2, 4)
-
-    def piece(across, member, c, start=0, count=CHUNK):
-        return abuf.at[across, pl.ds(c * CHUNK + start, count), pl.ds(al(member * ROWS, ROWS), ROWS)]
+    done = 1 + jnp.minimum(z, 4) // 2
+
+    def piece(across, member, c, start=0, count=PART):
+        return abuf.at[across, pl.ds(c * PART + start, count), pl.ds(al(member * ROWS, ROWS), ROWS)]
 
     def a_sends(c):
         part = piece(xh, j, c)
@@ -297,12 +301,12 @@
                 copy(part, part, acs.at[c, 0], acr.at[c, 0], core))
 
     def a_from_down(c):
-        part, half = piece(down_xh, opp, c), piece(down_xh, opp, c, 0, CHUNK // 2)
+        part, half = piece(down_xh, opp, c), piece(down_xh, opp, c, 0, PART // 2)
         return (copy(half, half, ars.at[c, 0], arr.at[c, 0], x_up),
                 copy(part, part, acs.at[c, 1], acr.at[c, 1], core))
 
     def a_from_up(c):
-        part, half = piece(up_xh, opp, c), piece(up_xh, opp, c, CHUNK // 2, CHUNK // 2)
+        part, half = piece(up_xh, opp, c), piece(up_xh, opp, c, PART // 2, PART // 2)
         return (copy(half, half, ars.at[c, 1], arr.at[c, 1], x_down),
                 copy(part, part, acs.at[c, 2], acr.at[c, 2], core))
 
@@ -310,20 +314,19 @@
         part = piece(1 - xh, j, c)
         return copy(part, part, acs.at[c, 3], acr.at[c, 3], core)
 
-    for c in range(2):
-        last_visit(c)
-        for h in range(c * 4, c * 4 + 4):
+    for c in range(4):
+        if c % 2 == 0:
+            last_visit(c // 2)
+        for h in range(c * 2, c * 2 + 2):
             lanes = slice(h * ROWS, (h + 1) * ROWS)
             o = (acc[:, lanes] / l_ref[:, lanes]).astype(jnp.bfloat16)
             a = jnp.dot(uvt[h * NOPE:(h + 1) * NOPE, :], o, preferred_element_type=jnp.float32)
             abuf[xh, h * NOPE:(h + 1) * NOPE, mine] = a.astype(jnp.bfloat16)
         for each in a_sends(c):
             each.start()
-        if c == 0:
-            @pl.when(z >= 1)
-            def _():
-                forward(done)
-    for c in range(2):
+        if c == 1:
+            forward(done)
+    for c in range(4):
         arrived(piece(down_xh, opp, c), axr.at[c, 0])
         for each in a_from_down(c):
             each.start()
@@ -331,16 +334,14 @@
         for each in a_from_up(c):
             each.start()
 
-    @pl.when(z <= 4)
-    def _():
-        forward(done + 1)
-
-    for c in range(2):
-        arrived(piece(1 - xh, j, c, 0, CHUNK // 2), arr.at[c, 0])
-        arrived(piece(1 - xh, j, c, CHUNK // 2, CHUNK // 2), arr.at[c, 1])
+    forward(done + 1)
+
+    for c in range(4):
+        arrived(piece(1 - xh, j, c, 0, PART // 2), arr.at[c, 0])
+        arrived(piece(1 - xh, j, c, PART // 2, PART // 2), arr.at[c, 1])
         a_across(c).start()
-    forward(jnp.minimum(done + 2, 5))
-    for c in range(2):
+    forward(done + 2)
+    for c in range(4):
         arrived(piece(xh, sib, c), acr.at[c, 0])
         arrived(piece(down_xh, opp_sib, c), acr.at[c, 1])
         arrived(piece(up_xh, opp_sib, c), acr.at[c, 2])
@@ -399,7 +400,7 @@
             f_copy(s).start()
 
     def reach(k):
-        @pl.when(k >= jnp.minimum(done + 3, 6))
+        @pl.when(k >= done + 3)
         def _():
             forward(k)
 
@@ -411,18 +412,20 @@
         reach(2 * g - 1)
         multiply([2 * g - 1, 2 * g])
 
-        @pl.when(g == 1)
+        @pl.when(g == 2)
         def _():
             gather(0)
 
-        @pl.when(g > 1)
-        def _():
-            gather(2 * g - 3)
-            gather(2 * g - 2)
+        @pl.when(g == 3)
+        def _():
+            gather(1)
+            gather(2)
 
     reach(6)
     multiply([7])
-    for s in range(5, 8):
+
+    @pl.loop(3, NZ)
+    def _(s):
         gather(s)
 
     for p in range(4):
@@ -432,11 +435,6 @@
                 arrived(fin.at[pl.ds((2 * p + b) * HALF, HALF), :], fr.at[2 * p + b])
     out_ref[...] = fin[...]
 
-    for k in range(1, NZ):
-        @pl.when(z + k < NZ)
-        def _():
-            z_copy(k).wait_send()
-
     @pl.loop(0, z + 1)
     def _(zs):
         @pl.when(zs < z)
@@ -455,7 +453,7 @@
         ring_up(u).wait_send()
         ring_down(u).wait_send()
 
-    for c in range(2):
+    for c in range(4):
         for each in a_sends(c) + a_from_down(c) + a_from_up(c) + (a_across(c),):
             each.wait_send()
 
@@ -502,9 +500,9 @@
             dma, dma,
             dma((7,)), dma((7,)),
             dma((7,)), dma((7,)),
-            dma((2, 2)), dma((2, 2)),
-            dma((2, 2)), dma((2, 2)),
-            dma((2, 4)), dma((2, 4)),
+            dma((4, 2)), dma((4, 2)),
+            dma((4, 2)), dma((4, 2)),
+            dma((4, 4)), dma((4, 4)),
             dma((NZ, 4)), dma((NZ, 4)),
             dma((NZ,)), dma((NZ,)),
         ],

time: 80.6 us -> 77.8 us (0.965)
  Pallas kernels: 78.7 us -> 75.9 us
    pallas_call x1, Pallas kernels: 78.7 us -> 75.9 us  [on_device(): pl.pallas_call(kernel, out_shape=jax.ShapeDtypeStruct((NZ * HALF, ROWS),...]
where the time goes in v5:
time: 77.8 us; the launch traced here: 77.7 us
  Pallas kernels  75.9 us (98%)
  local copies, waits for them, and re-layouts  1.76 us (2%)
    pallas_call x1, Pallas kernels, on_device(): pl.pallas_call(kernel, out_shape=jax.ShapeDtypeStruct((NZ * HALF, ROWS),...  75.9 us
    transpose x1, local copies, waits for them, and re-layouts, on_device(): return pl.pallas_call(kernel, out_shape=jax.ShapeDtypeStruct((NZ * HALF,...  1.76 us

profile of v5, /device:TPU:239, one launch (start us, length us, event | category | flops | bytes accessed | tf_op | source)
XLA Modules:
  0.0 77.7 jit_solution(116759854933610360)
XLA Ops:
  0.0 75.9 %layer.1 = bf16[896,128]{1,0:T(8,128)(2,1)} custom-call(bf16[128,1536]{1,0:T(8,128)(2,1)} %q_hbm.1, bf16[576,128]{1,0:T(8,128)(2,1)} %bitcast.6, f32[1,512]{1,0:T(1,128)} %bitcast.7, bf16[512,1024]{1,0:T(8,128)(2,1)} %uk_hbm.1, bf16[512,1024]{1,0:T(8,128)(2,1)} %uv_hbm.1, bf16[224,1024]{1,0:T(8,128)(2,1)} %bitcast.5), custom_call_target="tpu_custom_call" | custom-call | tf_op jit(solution)/shard_map/layer/pallas_call | solution.py:472
  75.9 1.8 %copy.7 = bf16[128,896]{1,0:T(8,128)(2,1)} copy(bf16[128,896]{0,1:T(8,128)(2,1)} %bitcast.4) | data formatting | bytes 458752 | tf_op jit(solution)/shard_map/transpose | solution.py:512

commit v6 on v5

--- a/solution.py
+++ b/solution.py
@@ -33,7 +33,7 @@
            q_ref, comp_ref, uk_ref, uv_ref, w_ref, loads,
            lat, ball, qt, uvt, m_ref, l_ref, acc, abuf, cbuf, rbuf, fsrc, fin,
            s1s, s1r, s2s, s2r, s3s, s3r, s4s, s4r, sws, swr, brs, brr, bls, blr,
-           axs, axr, ars, arr, acs, acr, cs, cr, fs, fr):
+           axs, axr, ars, arr, acr, cs, cr, fs, fr):
     ctx = lax.axis_index("ctx")
     head = lax.axis_index("head")
     z = ctx // 4
@@ -116,17 +116,17 @@
 
     def y_copy(zs, k):
         part = rows_of(zs, j, y * 32, 32)
-        return copy(part, part, s2s.at[zs, k - 1], s2r.at[zs, k - 1], (ctx, 2 * ((y + k) % 4) + xh))
+        return copy(part, part, s2s.at[zs], s2r.at[zs], (ctx, 2 * ((y + k) % 4) + xh))
 
     def x_copies(zs):
         low = rows_of(zs, j, 0, 64)
         high = rows_of(zs, j, 64, 64)
-        return (copy(low, low, s3s.at[zs, 0], s3r.at[zs, 0], x_up),
-                copy(high, high, s3s.at[zs, 1], s3r.at[zs, 1], x_down))
-
-    def core_copy(zs, member, slot):
+        return (copy(low, low, s3s.at[zs], s3r.at[zs], x_up),
+                copy(high, high, s3s.at[zs], s3r.at[zs], x_down))
+
+    def core_copy(zs, member, send):
         part = rows_of(zs, member, 0, ROWS)
-        return copy(part, part, s4s.at[zs, slot], s4r.at[zs, slot], core)
+        return copy(part, part, send.at[zs], s4r.at[zs], core)
 
     def stage1(d):
         zs = z - d
@@ -137,51 +137,58 @@
     def stage2(d, wait=True):
         zs = z - d
         if wait:
-            for k in range(1, 4):
-                arrived(rows_of(zs, j, ((y + 4 - k) % 4) * 32, 32), s2r.at[zs, k - 1])
+            arrived(rows_of(zs, j, 0, 96), s2r.at[zs])
         for each in x_copies(zs):
             each.start()
-        core_copy(zs, j, 0).start()
+        core_copy(zs, j, s3s).start()
 
     def stage3(d):
         zs = z - d
-        arrived(rows_of(zs, opp, 0, 64), s3r.at[zs, 0])
-        arrived(rows_of(zs, opp, 64, 64), s3r.at[zs, 1])
-        core_copy(zs, opp, 1).start()
+        arrived(rows_of(zs, opp, 0, ROWS), s3r.at[zs])
+        core_copy(zs, opp, s4s).start()
 
     def stage4(d):
         zs = z - d
-        arrived(rows_of(zs, sib, 0, ROWS), s4r.at[zs, 0])
-        arrived(rows_of(zs, opp_sib, 0, ROWS), s4r.at[zs, 1])
+        arrived(lat.at[zs, pl.ds(0, 2 * ROWS), :], s4r.at[zs])
 
     swap = copy(w_ref.at[pl.ds(al((1 - xh) * HALF, 16), HALF), :], ball.at[z, xh], sws, swr, over)
 
     def ring_up(u):
         part = ball.at[(z + NZ - u // 2) % NZ, (xh + u) % 2]
-        return copy(part, part, brs.at[u], brr.at[u], z_up)
+        return copy(part, part, brs, brr.at[u], z_up)
 
     def ring_down(u):
         part = ball.at[(z + u // 2) % NZ, (xh + u + u // 6) % 2]
-        return copy(part, part, bls.at[u], blr.at[u], z_down)
-
-    def ring_arrived(k):
+        return copy(part, part, bls, blr.at[u], z_down)
+
+    def pass_up(k):
         arrived(ball.at[(z + 7 - k // 2) % NZ, (xh + k) % 2], brr.at[k])
+
+        @pl.when(k < 5)
+        def _():
+            ring_up(k + 2).start()
+
+    def pass_down(k):
         arrived(ball.at[(z + 1 + k // 2) % NZ, (xh + k + k // 6) % 2], blr.at[k])
 
+        @pl.when(k < 4)
+        def _():
+            ring_down(k + 2).start()
+
+        @pl.when(k == 5)
+        def _():
+            ring_down(6).start()
+
     def forward(k):
-        ring_arrived(k)
-
-        @pl.when(k < 5)
-        def _():
-            ring_up(k + 2).start()
-
-        @pl.when(k < 4)
-        def _():
-            ring_down(k + 2).start()
-
-        @pl.when(k == 5)
-        def _():
-            ring_down(6).start()
+        @pl.when(z < 4)
+        def _():
+            pass_down(k)
+            pass_up(k)
+
+        @pl.when(z >= 4)
+        def _():
+            pass_up(k)
+            pass_down(k)
 
     def when_in(d, act):
         @pl.when(d <= z)
@@ -296,23 +303,23 @@
 
     def a_sends(c):
         part = piece(xh, j, c)
-        return (copy(part, part, axs.at[c, 0], axr.at[c, 0], x_up),
-                copy(part, part, axs.at[c, 1], axr.at[c, 1], x_down),
-                copy(part, part, acs.at[c, 0], acr.at[c, 0], core))
+        return (copy(part, part, axs, axr.at[c, 0], x_up),
+                copy(part, part, axs, axr.at[c, 1], x_down),
+                copy(part, part, axs, acr, core))
 
     def a_from_down(c):
         part, half = piece(down_xh, opp, c), piece(down_xh, opp, c, 0, PART // 2)
-        return (copy(half, half, ars.at[c, 0], arr.at[c, 0], x_up),
-                copy(part, part, acs.at[c, 1], acr.at[c, 1], core))
+        return (copy(half, half, ars, arr.at[c], x_up),
+                copy(part, part, ars, acr, core))
 
     def a_from_up(c):
         part, half = piece(up_xh, opp, c), piece(up_xh, opp, c, PART // 2, PART // 2)
-        return (copy(half, half, ars.at[c, 1], arr.at[c, 1], x_down),
-                copy(part, part, acs.at[c, 2], acr.at[c, 2], core))
+        return (copy(half, half, ars, arr.at[c], x_down),
+                copy(part, part, ars, acr, core))
 
     def a_across(c):
         part = piece(1 - xh, j, c)
-        return copy(part, part, acs.at[c, 3], acr.at[c, 3], core)
+        return copy(part, part, ars, acr, core)
 
     for c in range(4):
         if c % 2 == 0:
@@ -337,22 +344,17 @@
     forward(done + 1)
 
     for c in range(4):
-        arrived(piece(1 - xh, j, c, 0, PART // 2), arr.at[c, 0])
-        arrived(piece(1 - xh, j, c, PART // 2, PART // 2), arr.at[c, 1])
+        arrived(piece(1 - xh, j, c), arr.at[c])
         a_across(c).start()
     forward(done + 2)
-    for c in range(4):
-        arrived(piece(xh, sib, c), acr.at[c, 0])
-        arrived(piece(down_xh, opp_sib, c), acr.at[c, 1])
-        arrived(piece(up_xh, opp_sib, c), acr.at[c, 2])
-        arrived(piece(1 - xh, sib, c), acr.at[c, 3])
+    arrived(abuf.at[0], acr)
 
     def home(s):
         far = (s + 1) // 2
         return (z + NZ + far * (1 - 2 * (s % 2))) % NZ
 
     def c_copy(s, t):
-        return copy(cbuf.at[s, t], rbuf.at[s, y], cs.at[s, t], cr.at[s, y], (ctx, 2 * t + xh))
+        return copy(cbuf.at[s, t], rbuf.at[s, y], cs, cr.at[s], (ctx, 2 * t + xh))
 
     def each_copy(s, act):
         for t in range(4):
@@ -376,15 +378,13 @@
     spot = fin.at[pl.ds(al((2 * j + xh) * HALF, HALF), HALF), :]
 
     def f_copy(s):
-        return copy(fsrc.at[s], spot, fs.at[s], fr.at[2 * j + xh], (base + y, home(s)))
+        return copy(fsrc.at[s], spot, fs, fr, (base + y, home(s)))
 
     def is_here(s):
         return (y == j) & (home(s) == head)
 
     def gather(s):
-        for k in range(1, 4):
-            peer = (y + k) % 4
-            arrived(rbuf.at[s, peer], cr.at[s, peer])
+        arrived(rbuf.at[s, pl.ds(0, 3)], cr.at[s])
         total = cbuf[s, y].astype(jnp.float32)
         for k in range(1, 4):
             total = total + rbuf[s, (y + k) % 4].astype(jnp.float32)
@@ -412,14 +412,10 @@
         reach(2 * g - 1)
         multiply([2 * g - 1, 2 * g])
 
-        @pl.when(g == 2)
-        def _():
-            gather(0)
-
         @pl.when(g == 3)
         def _():
-            gather(1)
-            gather(2)
+            for s in range(3):
+                gather(s)
 
     reach(6)
     multiply([7])
@@ -428,42 +424,41 @@
     def _(s):
         gather(s)
 
-    for p in range(4):
-        for b in range(2):
-            @pl.when((p != j) | (j != y) | (b != xh))
-            def _():
-                arrived(fin.at[pl.ds((2 * p + b) * HALF, HALF), :], fr.at[2 * p + b])
+    @pl.when(j == y)
+    def _():
+        arrived(fin.at[pl.ds(0, 7 * HALF), :], fr)
+
+    @pl.when(j != y)
+    def _():
+        arrived(fin, fr)
+
     out_ref[...] = fin[...]
 
     @pl.loop(0, z + 1)
     def _(zs):
         @pl.when(zs < z)
         def _():
-            for k in range(1, 4):
-                y_copy(zs, k).wait_send()
-        for each in x_copies(zs):
-            each.wait_send()
-        core_copy(zs, j, 0).wait_send()
-        core_copy(zs, opp, 1).wait_send()
+            left(rows_of(zs, j, 0, 96), s2s.at[zs])
+        left(lat.at[zs, pl.ds(0, 2 * ROWS), :], s3s.at[zs])
+        left(rows_of(zs, opp, 0, ROWS), s4s.at[zs])
 
     swap.wait_send()
 
-    @pl.loop(0, 7)
-    def _(u):
-        ring_up(u).wait_send()
-        ring_down(u).wait_send()
-
-    for c in range(4):
-        for each in a_sends(c) + a_from_down(c) + a_from_up(c) + (a_across(c),):
-            each.wait_send()
-
-    @pl.loop(0, NZ)
-    def _(s):
-        each_copy(s, lambda each: each.wait_send())
-
-        @pl.when(jnp.logical_not(is_here(s)))
-        def _():
-            f_copy(s).wait_send()
+    left(ball.at[pl.ds(0, 7), 0], brs)
+    left(ball.at[pl.ds(0, 7), 0], bls)
+
+    left(abuf.at[0, pl.ds(0, 768), :], axs)
+    left(abuf.at[0], ars)
+
+    left(cbuf.at[:, pl.ds(0, 3)], cs)
+
+    @pl.when(j == y)
+    def _():
+        left(fsrc.at[pl.ds(0, 7)], fs)
+
+    @pl.when(j != y)
+    def _():
+        left(fsrc, fs)
 
 
 def on_device(queries, compressed, latent_gain, w_uk, w_uv, w_out):
@@ -494,17 +489,16 @@
             pltpu.VMEM((NZ, HALF, ROWS), bf),
             pltpu.VMEM((NZ * HALF, ROWS), bf),
             dma((NZ,)), dma((NZ,)),
-            dma((NZ, 3)), dma((NZ, 3)),
-            dma((NZ, 2)), dma((NZ, 2)),
-            dma((NZ, 2)), dma((NZ, 2)),
+            dma((NZ,)), dma((NZ,)),
+            dma((NZ,)), dma((NZ,)),
+            dma((NZ,)), dma((NZ,)),
             dma, dma,
-            dma((7,)), dma((7,)),
-            dma((7,)), dma((7,)),
-            dma((4, 2)), dma((4, 2)),
-            dma((4, 2)), dma((4, 2)),
-            dma((4, 4)), dma((4, 4)),
-            dma((NZ, 4)), dma((NZ, 4)),
-            dma((NZ,)), dma((NZ,)),
+            dma, dma((7,)),
+            dma, dma((7,)),
+            dma, dma((4, 2)),
+            dma, dma((4,)), dma,
+            dma, dma((NZ,)),
+            dma, dma,
         ],
         compiler_params=pltpu.CompilerParams(
             collective_id=0, has_side_effects=True, vmem_limit_bytes=56 * 1024 * 1024),

time: 77.8 us -> 75.7 us (0.973)
  Pallas kernels: 75.9 us -> 73.8 us
    pallas_call x1, Pallas kernels: 75.9 us -> 73.8 us  [on_device(): pl.pallas_call(kernel, out_shape=jax.ShapeDtypeStruct((NZ * HALF, ROWS),...]
where the time goes in v6:
time: 75.7 us; the launch traced here: 75.6 us
  Pallas kernels  73.8 us (97%)
  local copies, waits for them, and re-layouts  1.76 us (2%)
    pallas_call x1, Pallas kernels, on_device(): pl.pallas_call(kernel, out_shape=jax.ShapeDtypeStruct((NZ * HALF, ROWS),...  73.8 us
    transpose x1, local copies, waits for them, and re-layouts, on_device(): return pl.pallas_call(kernel, out_shape=jax.ShapeDtypeStruct((NZ * HALF,...  1.76 us

profile of v6, /device:TPU:239, one launch (start us, length us, event | category | flops | bytes accessed | tf_op | source)
XLA Modules:
  0.0 75.6 jit_solution(3914182250102714065)
XLA Ops:
  0.0 73.8 %layer.1 = bf16[896,128]{1,0:T(8,128)(2,1)} custom-call(bf16[128,1536]{1,0:T(8,128)(2,1)} %q_hbm.1, bf16[576,128]{1,0:T(8,128)(2,1)} %bitcast.6, f32[1,512]{1,0:T(1,128)} %bitcast.7, bf16[512,1024]{1,0:T(8,128)(2,1)} %uk_hbm.1, bf16[512,1024]{1,0:T(8,128)(2,1)} %uv_hbm.1, bf16[224,1024]{1,0:T(8,128)(2,1)} %bitcast.5), custom_call_target="tpu_custom_call" | custom-call | tf_op jit(solution)/shard_map/layer/pallas_call | solution.py:467
  73.8 1.8 %copy.7 = bf16[128,896]{1,0:T(8,128)(2,1)} copy(bf16[128,896]{0,1:T(8,128)(2,1)} %bitcast.4) | data formatting | bytes 458752 | tf_op jit(solution)/shard_map/transpose | solution.py:506

commit v7 on v6

--- a/solution.py
+++ b/solution.py
@@ -221,16 +221,13 @@
             z_copy(k).wait_send()
     ring_up(0).start()
     ring_down(0).start()
+    stage3(0)
     arrived(ball.at[z, 1 - xh], swr)
     ring_up(1).start()
     ring_down(1).start()
-    when_in(1, stage2)
     when_in(4, stage1)
     when_in(5, stage1)
-    when_in(2, stage2)
-    stage3(0)
-    when_in(3, stage2)
-    forward(0)
+    when_in(1, stage2)
 
     def visit(zs, first, chunk=None):
         block = lat[zs]
@@ -269,21 +266,21 @@
         else:
             rest(score(chunk), chunk)
 
-    def ahead(i):
-        when_in(i + 6, stage1)
-        when_in(i + 4, stage2)
-
     stage4(0)
     visit(z, True)
+    when_in(2, stage2)
+    when_in(6, stage1)
+    when_in(3, stage2)
     when_in(1, stage3)
-    ahead(0)
+    forward(0)
 
     @pl.loop(1, z)
     def _(i):
         when_in(i + 1, stage3)
+        when_in(i + 6, stage1)
+        when_in(i + 3, stage2)
         stage4(i)
         visit(z - i, False)
-        ahead(i)
 
         @pl.when(jnp.where(z >= 5, (i == 2) | (i == 4), i % 2 == 1))
         def _():

time: 75.7 us -> 74 us (0.978)
  Pallas kernels: 73.8 us -> 71.4 us
    pallas_call x1, Pallas kernels: 73.8 us -> 71.4 us  [on_device(): pl.pallas_call(kernel, out_shape=jax.ShapeDtypeStruct((NZ * HALF, ROWS),...]
where the time goes in v7:
time: 74 us; the launch traced here: 73.2 us
  Pallas kernels  71.4 us (96%)
  local copies, waits for them, and re-layouts  1.76 us (2%)
    pallas_call x1, Pallas kernels, on_device(): pl.pallas_call(kernel, out_shape=jax.ShapeDtypeStruct((NZ * HALF, ROWS),...  71.4 us
    transpose x1, local copies, waits for them, and re-layouts, on_device(): return pl.pallas_call(kernel, out_shape=jax.ShapeDtypeStruct((NZ * HALF,...  1.76 us

profile of v7, /device:TPU:239, one launch (start us, length us, event | category | flops | bytes accessed | tf_op | source)
XLA Modules:
  0.0 73.2 jit_solution(3359810416181766158)
XLA Ops:
  0.0 71.4 %layer.1 = bf16[896,128]{1,0:T(8,128)(2,1)} custom-call(bf16[128,1536]{1,0:T(8,128)(2,1)} %q_hbm.1, bf16[576,128]{1,0:T(8,128)(2,1)} %bitcast.6, f32[1,512]{1,0:T(1,128)} %bitcast.7, bf16[512,1024]{1,0:T(8,128)(2,1)} %uk_hbm.1, bf16[512,1024]{1,0:T(8,128)(2,1)} %uv_hbm.1, bf16[224,1024]{1,0:T(8,128)(2,1)} %bitcast.5), custom_call_target="tpu_custom_call" | custom-call | tf_op jit(solution)/shard_map/layer/pallas_call | solution.py:464
  71.4 1.8 %copy.7 = bf16[128,896]{1,0:T(8,128)(2,1)} copy(bf16[128,896]{0,1:T(8,128)(2,1)} %bitcast.4) | data formatting | bytes 458752 | tf_op jit(solution)/shard_map/transpose | solution.py:503

commit v8 on v7

--- a/solution.py
+++ b/solution.py
@@ -197,6 +197,8 @@
 
     swap.start()
     stage2(0, wait=False)
+    ring_up(0).start()
+    ring_down(0).start()
 
     def absorb(h):
         lanes = slice(h * ROWS, (h + 1) * ROWS)
@@ -219,8 +221,6 @@
         @pl.when(z + k < NZ)
         def _():
             z_copy(k).wait_send()
-    ring_up(0).start()
-    ring_down(0).start()
     stage3(0)
     arrived(ball.at[z, 1 - xh], swr)
     ring_up(1).start()

time: 74 us -> 72.9 us (0.985)
  no operation moved by 1% of the time
where the time goes in v8:
time: 72.9 us; the launch traced here: 72.7 us
  Pallas kernels  70.9 us (97%)
  local copies, waits for them, and re-layouts  1.76 us (2%)
    pallas_call x1, Pallas kernels, on_device(): pl.pallas_call(kernel, out_shape=jax.ShapeDtypeStruct((NZ * HALF, ROWS),...  70.9 us
    transpose x1, local copies, waits for them, and re-layouts, on_device(): return pl.pallas_call(kernel, out_shape=jax.ShapeDtypeStruct((NZ * HALF,...  1.76 us

profile of v8, /device:TPU:239, one launch (start us, length us, event | category | flops | bytes accessed | tf_op | source)
XLA Modules:
  0.0 72.7 jit_solution(7876115301388423987)
XLA Ops:
  0.0 70.9 %layer.1 = bf16[896,128]{1,0:T(8,128)(2,1)} custom-call(bf16[128,1536]{1,0:T(8,128)(2,1)} %q_hbm.1, bf16[576,128]{1,0:T(8,128)(2,1)} %bitcast.6, f32[1,512]{1,0:T(1,128)} %bitcast.7, bf16[512,1024]{1,0:T(8,128)(2,1)} %uk_hbm.1, bf16[512,1024]{1,0:T(8,128)(2,1)} %uv_hbm.1, bf16[224,1024]{1,0:T(8,128)(2,1)} %bitcast.5), custom_call_target="tpu_custom_call" | custom-call | tf_op jit(solution)/shard_map/layer/pallas_call | solution.py:464
  71.0 1.8 %copy.7 = bf16[128,896]{1,0:T(8,128)(2,1)} copy(bf16[128,896]{0,1:T(8,128)(2,1)} %bitcast.4) | data formatting | bytes 458752 | tf_op jit(solution)/shard_map/transpose | solution.py:503

commit v9 on v8

--- a/solution.py
+++ b/solution.py
@@ -32,7 +32,7 @@
 def kernel(q_hbm, comp_hbm, gain_ref, uk_hbm, uv_hbm, w_hbm, out_ref,
            q_ref, comp_ref, uk_ref, uv_ref, w_ref, loads,
            lat, ball, qt, uvt, m_ref, l_ref, acc, abuf, cbuf, rbuf, fsrc, fin,
-           s1s, s1r, s2s, s2r, s3s, s3r, s4s, s4r, sws, swr, brs, brr, bls, blr,
+           s1s, s1r, s2s, s2r, s3r, s4r, sws, swr, brs, brr, bls, blr,
            axs, axr, ars, arr, acr, cs, cr, fs, fr):
     ctx = lax.axis_index("ctx")
     head = lax.axis_index("head")
@@ -121,8 +121,8 @@
     def x_copies(zs):
         low = rows_of(zs, j, 0, 64)
         high = rows_of(zs, j, 64, 64)
-        return (copy(low, low, s3s.at[zs], s3r.at[zs], x_up),
-                copy(high, high, s3s.at[zs], s3r.at[zs], x_down))
+        return (copy(low, low, s2s.at[zs], s3r.at[zs], x_up),
+                copy(high, high, s2s.at[zs], s3r.at[zs], x_down))
 
     def core_copy(zs, member, send):
         part = rows_of(zs, member, 0, ROWS)
@@ -140,12 +140,12 @@
             arrived(rows_of(zs, j, 0, 96), s2r.at[zs])
         for each in x_copies(zs):
             each.start()
-        core_copy(zs, j, s3s).start()
+        core_copy(zs, j, s2s).start()
 
     def stage3(d):
         zs = z - d
         arrived(rows_of(zs, opp, 0, ROWS), s3r.at[zs])
-        core_copy(zs, opp, s4s).start()
+        core_copy(zs, opp, s2s).start()
 
     def stage4(d):
         zs = z - d
@@ -217,10 +217,6 @@
     uvt[...] = uv_ref[...].T
     for d in range(1, 4):
         when_in(d, stage1)
-    for k in range(1, NZ):
-        @pl.when(z + k < NZ)
-        def _():
-            z_copy(k).wait_send()
     stage3(0)
     arrived(ball.at[z, 1 - xh], swr)
     ring_up(1).start()
@@ -431,13 +427,20 @@
 
     out_ref[...] = fin[...]
 
+    for k in range(1, NZ):
+        @pl.when(z + k < NZ)
+        def _():
+            z_copy(k).wait_send()
+
     @pl.loop(0, z + 1)
     def _(zs):
         @pl.when(zs < z)
         def _():
-            left(rows_of(zs, j, 0, 96), s2s.at[zs])
-        left(lat.at[zs, pl.ds(0, 2 * ROWS), :], s3s.at[zs])
-        left(rows_of(zs, opp, 0, ROWS), s4s.at[zs])
+            left(lat.at[zs, pl.ds(0, 480), :], s2s.at[zs])
+
+        @pl.when(zs == z)
+        def _():
+            left(lat.at[zs, pl.ds(0, 384), :], s2s.at[zs])
 
     swap.wait_send()
 
@@ -488,7 +491,6 @@
             dma((NZ,)), dma((NZ,)),
             dma((NZ,)), dma((NZ,)),
             dma((NZ,)), dma((NZ,)),
-            dma((NZ,)), dma((NZ,)),
             dma, dma,
             dma, dma((7,)),
             dma, dma((7,)),

time: 72.9 us -> 72.7 us (level)
  no operation moved by 1% of the time
where the time goes in v9:
time: 72.7 us; the launch traced here: 72.6 us
  Pallas kernels  70.8 us (97%)
  local copies, waits for them, and re-layouts  1.76 us (2%)
    pallas_call x1, Pallas kernels, on_device(): pl.pallas_call(kernel, out_shape=jax.ShapeDtypeStruct((NZ * HALF, ROWS),...  70.8 us
    transpose x1, local copies, waits for them, and re-layouts, on_device(): return pl.pallas_call(kernel, out_shape=jax.ShapeDtypeStruct((NZ * HALF,...  1.76 us

profile of v9, /device:TPU:239, one launch (start us, length us, event | category | flops | bytes accessed | tf_op | source)
XLA Modules:
  0.0 72.6 jit_solution(7858471612021056334)
XLA Ops:
  0.0 70.8 %layer.1 = bf16[896,128]{1,0:T(8,128)(2,1)} custom-call(bf16[128,1536]{1,0:T(8,128)(2,1)} %q_hbm.1, bf16[576,128]{1,0:T(8,128)(2,1)} %bitcast.6, f32[1,512]{1,0:T(1,128)} %bitcast.7, bf16[512,1024]{1,0:T(8,128)(2,1)} %uk_hbm.1, bf16[512,1024]{1,0:T(8,128)(2,1)} %uv_hbm.1, bf16[224,1024]{1,0:T(8,128)(2,1)} %bitcast.5), custom_call_target="tpu_custom_call" | custom-call | tf_op jit(solution)/shard_map/layer/pallas_call | solution.py:467
  70.8 1.8 %copy.7 = bf16[128,896]{1,0:T(8,128)(2,1)} copy(bf16[128,896]{0,1:T(8,128)(2,1)} %bitcast.4) | data formatting | bytes 458752 | tf_op jit(solution)/shard_map/transpose | solution.py:505
